TPU v7x, 32 devices: a whole 2x2x4 slice. The times are simulated.
32 devices in a mesh: seq: 8 (over z, x), head: 4 (over y, core).
Axes of the slice: x: 2, y: 2, z: 4, core: 2. Of those that a mesh axis runs over, the one named last changes fastest.
Arguments:
- queries: bfloat16 [2048, 8192], P('seq', 'head'), may hold values from -6 to 6
- key_rows: bfloat16 [2048, 8192], P('seq', 'head'), may hold values from -6 to 6
- value_rows: bfloat16 [2048, 8192], P('seq', 'head'), may hold values from -160 to 160
- log_decay: float32 [2048, 64], P('seq', 'head'), may hold values from -0.5 to 0, as said below
- gate_input: bfloat16 [2048, 8192], P('seq', 'head'), may hold values from -12 to 12
- out_gain: float32 [8192], P('head'), may hold values from 0.1 to 1.9
- prior_state: float32 [64, 128, 128], P('head'), may hold values from -192 to 192
- out_grad: bfloat16 [2048, 8192], P('seq', 'head'), may hold values from -6 to 6
Outputs:
- attended: bfloat16 [2048, 8192], P('seq', 'head')
- grad_query: bfloat16 [2048, 8192], P('seq', 'head')
- grad_key: bfloat16 [2048, 8192], P('seq', 'head')
- grad_value: bfloat16 [2048, 8192], P('seq', 'head')
- grad_gate: bfloat16 [2048, 8192], P('seq', 'head')
Inputs may be any that keep to these rules, and one draw needn't show every extreme that they name: `log_decay`: every entry is negative; at each token a head's state is multiplied by exp(entry).
All inputs are finite; a program needn't handle non-finite values.
Results may differ from a plain program's by a relative error of at most 0.012.
Values sent between devices are 32-bit elements; how exact they have to be, the bound alone decides.
A program may use at most 64 MiB of HBM per device.

v0:
```python
import jax
import jax.numpy as jnp
from jax import lax
from jax.sharding import PartitionSpec as P

BLK = 256
D = 8192


epsilon = 1e-06


def prefix(shard, axis, combine, identity, reverse):
    count, here = (lax.axis_size(axis), lax.axis_index(axis))
    everything = jax.tree.map(lambda part: lax.all_gather(part, axis), shard)
    start = jax.tree.map(
        lambda part, zero: jnp.broadcast_to(jnp.asarray(zero, part.dtype), part.shape),
        shard,
        identity,
    )

    def lap(k, before):
        at = count - 1 - k if reverse else k
        reached = at > here if reverse else at < here
        new = combine(before, jax.tree.map(lambda part: part[at], everything))
        return jax.tree.map(lambda a, b: jnp.where(reached, a, b), new, before)

    return lax.fori_loop(0, count, lap, start)


def decay_tables(decay_block):
    running = jnp.cumsum(decay_block, axis=0)
    closing = running[-1]
    spread = running.T[:, :, None] - running.T[:, None, :]
    causal = jnp.arange(decay_block.shape[0])[:, None] >= jnp.arange(decay_block.shape[0])[None, :]
    weights = jnp.where(causal[None], jnp.exp(jnp.minimum(spread, 0.0)), 0.0)
    return (running, closing, weights)


def split_parts(wide):
    upper = wide.astype(jnp.bfloat16)
    lower = (wide - upper.astype(jnp.float32)).astype(jnp.bfloat16)
    return (upper, lower)


def state_product(form, left, right):
    if left.dtype == jnp.float32:
        upper, lower = split_parts(left)
        return jnp.einsum(form, upper, right, preferred_element_type=jnp.float32) + jnp.einsum(
            form, lower, right, preferred_element_type=jnp.float32
        )
    upper, lower = split_parts(right)
    return jnp.einsum(form, left, upper, preferred_element_type=jnp.float32) + jnp.einsum(
        form, left, lower, preferred_element_type=jnp.float32
    )


def mixing_of(query_block, key_block, weights):
    scores = jnp.einsum("the,she->hts", query_block, key_block, preferred_element_type=jnp.float32)
    return (scores * weights).astype(jnp.bfloat16)


def chain_states(earlier, later):
    return (earlier[0] + later[0], jnp.exp(later[0])[:, None, None] * earlier[1] + later[1])


def local_forward(carried, inputs):
    query_block, key_block, value_block, decay_block = inputs
    running, closing, weights = decay_tables(decay_block)
    mixing = mixing_of(query_block, key_block, weights)
    within = jnp.einsum("hts,she->the", mixing, value_block, preferred_element_type=jnp.float32)
    across = jnp.exp(running)[:, :, None] * state_product("the,hef->thf", query_block, carried)
    remain = jnp.exp(closing[None, :] - running)
    updated = jnp.exp(closing)[:, None, None] * carried + state_product(
        "she,shf->hef", key_block.astype(jnp.float32) * remain[:, :, None], value_block
    )
    return (updated, (within + across, carried, mixing))


def backward_core(returned, inputs, tables, mixing):
    query_block, key_block, value_block, grad_rows, decay_block, opening = inputs[:6]
    running, closing, weights = tables
    grad_scores = jnp.einsum(
        "thf,shf->hts", grad_rows, value_block, preferred_element_type=jnp.float32
    )
    grad_mixing = (grad_scores * weights).astype(jnp.bfloat16)
    grad_q = jnp.einsum(
        "hts,she->the", grad_mixing, key_block, preferred_element_type=jnp.float32
    ) + jnp.exp(running)[:, :, None] * state_product("thf,hef->the", grad_rows, opening)
    remain = jnp.exp(closing[None, :] - running)[:, :, None]
    grad_k = jnp.einsum(
        "hts,the->she", grad_mixing, query_block, preferred_element_type=jnp.float32
    ) + remain * state_product("shf,hef->she", value_block, returned)
    grad_v = jnp.einsum(
        "hts,thf->shf", mixing, grad_rows, preferred_element_type=jnp.float32
    ) + remain * state_product("she,hef->shf", key_block, returned)
    summed = state_product(
        "the,thf->hef", query_block.astype(jnp.float32) * jnp.exp(running)[:, :, None], grad_rows
    )
    updated = summed + jnp.exp(closing)[:, None, None] * returned
    return (updated, (grad_q, grad_k, grad_v))


def shards(queries, key_rows, value_rows, log_decay, gate_input, out_gain, prior_state, out_grad):
    length, features = queries.shape
    head_count = log_decay.shape[1]
    head_size = features // head_count
    blocks = length // BLK
    block_shape = (blocks, BLK, head_count, head_size)
    token_shape = (length, head_count, head_size)
    query_all = queries.reshape(block_shape)
    key_all = key_rows.reshape(block_shape)
    value_all = value_rows.reshape(block_shape)
    decay_all = log_decay.reshape(blocks, BLK, head_count)
    zero_state = jnp.zeros((head_count, head_size, head_size), jnp.float32)
    zero_decay = jnp.zeros((head_count,), jnp.float32)
    local_state, (context_parts, openings, kept_mixing) = lax.scan(
        local_forward, zero_state, (query_all, key_all, value_all, decay_all)
    )
    through_dev = jnp.cumsum(log_decay, axis=0)
    decay_sum = through_dev[-1]
    prefix_decay, prefix_state = prefix(
        (decay_sum, local_state), "seq", chain_states, (zero_decay, zero_state), False
    )
    incoming = prefix_state + jnp.exp(prefix_decay)[:, None, None] * prior_state
    query_rows = queries.reshape(token_shape)
    context = context_parts.reshape(token_shape) + jnp.exp(through_dev)[:, :, None] * state_product(
        "the,hef->thf", query_rows, incoming
    )
    merged = context.reshape(length, features)
    squares = lax.psum(jnp.sum(merged * merged, axis=1), "head")
    inverse = lax.rsqrt(squares / D + epsilon)
    normed = merged * inverse[:, None]
    opened = jax.nn.sigmoid(gate_input.astype(jnp.float32))
    attended = (normed * out_gain * opened).astype(jnp.bfloat16)
    grad_wide = out_grad.astype(jnp.float32)
    grad_gate = (grad_wide * normed * out_gain * opened * (1.0 - opened)).astype(jnp.bfloat16)
    grad_norm = grad_wide * out_gain * opened
    row_dot = lax.psum(jnp.sum(merged * grad_norm, axis=1), "head")
    grad_merged = (
        inverse[:, None] * grad_norm - merged * (inverse * inverse * inverse * row_dot / D)[:, None]
    )
    grad_context = grad_merged.astype(jnp.bfloat16)
    grad_all = grad_context.reshape(block_shape)
    inputs_all = (query_all, key_all, value_all, grad_all, decay_all, openings)

    def backward_step(returned, inputs):
        return backward_core(returned, inputs, decay_tables(inputs[4]), inputs[6])

    local_returned, (grad_q_parts, grad_k_parts, grad_v_parts) = lax.scan(
        backward_step, zero_state, inputs_all + (kept_mixing,), reverse=True
    )
    grad_rows_all = grad_context.reshape(token_shape)
    grad_query = grad_q_parts.reshape(token_shape) + jnp.exp(through_dev)[
        :, :, None
    ] * state_product("thf,hef->the", grad_rows_all, incoming)
    suffix_decay, outgoing = prefix(
        (decay_sum, local_returned), "seq", chain_states, (zero_decay, zero_state), True
    )
    remain = jnp.exp(decay_sum[None, :] - through_dev)[:, :, None]
    value_tokens = value_rows.reshape(token_shape)
    key_tokens = key_rows.reshape(token_shape)
    grad_key = grad_k_parts.reshape(token_shape) + remain * state_product(
        "shf,hef->she", value_tokens, outgoing
    )
    grad_value = grad_v_parts.reshape(token_shape) + remain * state_product(
        "she,hef->shf", key_tokens, outgoing
    )
    return (
        attended,
        grad_query.reshape(length, features).astype(jnp.bfloat16),
        grad_key.reshape(length, features).astype(jnp.bfloat16),
        grad_value.reshape(length, features).astype(jnp.bfloat16),
        grad_gate,
    )


def solution(mesh):
    return jax.shard_map(
        shards,
        mesh=mesh,
        in_specs=(
            P("seq", "head"),
            P("seq", "head"),
            P("seq", "head"),
            P("seq", "head"),
            P("seq", "head"),
            P("head"),
            P("head", None, None),
            P("seq", "head"),
        ),
        out_specs=(
            P("seq", "head"),
            P("seq", "head"),
            P("seq", "head"),
            P("seq", "head"),
            P("seq", "head"),
        ),
        check_vma=False,
    )
```

profile of v0, /device:TPU:0, one launch (start us, length us, event | category | flops | bytes accessed | tf_op | source)
XLA Modules:
  0.0 332.3 jit_solution(9240462647475877270)
XLA Ops:
  7.2 0.8 copy_bitcast_fusion.1
  8.0 0.6 reduce-window.14
  8.6 0.2 slice_reduce_fusion
  8.8 0.1 fusion.74
  8.9 0.2 slice_reduce_fusion.1
  9.1 0.1 bitcast_exponential_fusion.1
  9.2 1.5 copy.131
  10.7 0.4 fusion.36
  11.1 1.5 fusion.30
  12.7 1.5 copy.130
  14.2 22.2 %all-gather.2 = f32[8,1,16]{2,1,0:T(1,128)S(1)} all-gather(f32[1,1,16]{2,1,0:T(1,128)S(1)} %bitcast.198), channel_id=1, replica_groups=mesh['seq'=8,'head'=4] {'seq'}, dimensions={0}, use_global_device_ids=true | all-gather | bytes 576 | tf_op jit(solution)/shard_map/all_gather | solution.py:15
  36.5 1.5 multiply_convert_fusion.1
  38.0 1.3 copy-done.8
  39.3 2.2 fusion.38
  41.5 98.9 %all-gather.6.cloned.1.call-done = f32[128,128,128]{2,1,0:T(8,128)} async-done(((f32[16,128,128]{2,1,0:T(8,128)}), f32[128,128,128]{2,1,0:T(8,128)}) %all-gather.6.cloned.1.call-update) | async-done | bytes 8388624 | tf_op jit(solution)/shard_map/all_gather | solution.py:15
  140.4 12.0 %while.21 = (s32[]{:T(128)}, f32[16]{0:T(128)S(1)}, f32[16,128,128]{2,1,0:T(8,128)S(1)}, s32[]{:T(128)}, f32[8,16]{1,0:T(8,128)S(1)}, /*index=5*/f32[8,16,128,128]{3,2,1,0:T(8,128)}, s32[]{:T(128)}, s32[]{:T(128)}) while((s32[]{:T(128)}, f32[16]{0:T(128)S(1)}, f32[16,128,128]{2,1,0:T(8,128)S(1)}, s32[]{:T(128)}, ...), condition=%wide.region_3.4_spmd.clone, body=%wide.region_2.3_spmd.clone.sunk | while | flops 1048628 | bytes 3146171 | solution.py:28
  140.4 1.5 fusion.118
  141.9 1.5 fusion.118
  143.4 1.5 fusion.118
  144.9 1.5 fusion.118
  146.5 1.5 fusion.118
  148.0 1.5 fusion.118
  149.5 1.5 fusion.118
  151.0 1.5 fusion.118
  152.5 1.6 subtract_convert_fusion.6
  154.0 0.5 fusion.77
  154.6 0.5 fusion.76
  155.1 1.1 copy-done.7
  156.1 2.1 multiply_reduce_fusion.1
  158.3 3.0 copy.144
  161.3 2.6 multiply_reduce_fusion
  163.9 6.3 %all-reduce = (f32[256]{0:T(256)S(1)}, f32[256]{0:T(256)S(1)}) all-reduce(f32[256]{0:T(256)S(1)} %get-tuple-element.409, f32[256]{0:T(256)S(1)} %multiply_reduce_fusion), channel_id=1, replica_groups=mesh['seq'=8,'head'=4] {'head'}, use_global_device_ids=true, to_apply=%region_5.6 | all-reduce | flops 512 | bytes 4096 | tf_op jit(solution)/shard_map/psum | solution.py:131
  170.2 5.0 %fusion.6 = (bf16[256,2048]{1,0:T(8,128)(2,1)}, bf16[256,2048]{1,0:T(8,128)(2,1)}, bf16[256,2048]{1,0:T(8,128)(2,1)}) fusion(bf16[256,2048]{1,0:T(8,128)(2,1)S(1)} %copy-done.15, f32[256,2048]{1,0:T(8,128)} %copy.144, f32[2048]{0:T(1024)S(1)} %copy-done.16, f32[256]{0:T(256)S(1)} %get-tuple-element.408, bf16[256,2048]{1,0:T(8,128)(2,1)} %param.16, ...), kind=kLoop, calls=%fused_computation.18 | loop fusion | flops 11010048 | bytes 7350272 | tf_op jit(solution)/shard_map/convert_element_type | solution.py:137
  175.2 1.5 copy.182
  176.7 0.4 fusion.37
  177.2 1.4 fusion.33
  178.7 1.9 fusion.80
  180.6 0.4 fusion.79
  181.0 1.6 multiply_convert_fusion
  182.6 0.8 fusion.78
  183.4 0.5 copy-done.9
  183.9 1.6 fusion.14
  185.6 2.3 copy.165
  187.9 3.9 %fusion.81 = f32[16,128,256]{2,1,0:T(8,128)} fusion(bf16[256,16,128]{0,2,1:T(8,128)(2,1)} %bitcast.180, bf16[16,256,256]{2,1,0:T(8,128)(2,1)} %copy-done.8), kind=kOutput, calls=%fused_computation.113 | convolution fusion | flops 268435456 | bytes 5242880 | tf_op jit(solution)/shard_map/while/body/eval_jaxpr/hts,thf->shf/dot_general | solution.py:94
  191.7 1.8 fusion.82
  193.5 108.1 %all-gather.8.cloned.1.call-done = f32[128,128,128]{2,1,0:T(8,128)} async-done(((f32[16,128,128]{2,1,0:T(8,128)}), f32[128,128,128]{2,1,0:T(8,128)}) %all-gather.8.cloned.1.call-update) | async-done | bytes 8388624 | tf_op jit(solution)/shard_map/all_gather | solution.py:15
  301.7 12.1 %while.22 = (s32[]{:T(128)}, f32[16,128,128]{2,1,0:T(8,128)S(1)}, s32[]{:T(128)}, f32[8,16]{1,0:T(8,128)S(1)}, f32[8,16,128,128]{3,2,1,0:T(8,128)}, /*index=5*/s32[]{:T(128)}, s32[]{:T(128)}, s32[]{:T(128)}, s32[]{:T(128)}) while((s32[]{:T(128)}, f32[16,128,128]{2,1,0:T(8,128)S(1)}, s32[]{:T(128)}, f32[8,16]{1,0:T(8,128)S(1)}, ...), condition=%wide.region_9.10_spmd.clone, body=%wide.region_8.9_spmd.clone.sunk | while | flops 1048584 | bytes 3146095 | solution.py:28
  301.7 1.5 fusion.119
  303.3 1.5 fusion.119
  304.8 1.5 fusion.119
  306.3 1.5 fusion.119
  307.8 1.5 fusion.119
  309.3 1.5 fusion.119
  310.8 1.5 fusion.119
  312.3 1.5 fusion.119
  313.8 1.8 fusion.66
  315.6 0.4 fusion.40
  316.1 0.5 fusion.42
  316.5 1.8 fusion.69
  318.3 0.1 copy-done.11
  318.4 0.8 fusion.11
  319.2 1.4 copy.166
  320.6 3.4 %fusion.8 = bf16[256,16,128]{0,2,1:T(8,128)(2,1)S(1)} fusion(f32[16,128,256]{2,1,0:T(8,128)} %fusion.81, f32[16,128,256]{2,1,0:T(8,128)} %fusion.66, f32[16,128,256]{2,1,0:T(8,128)} %fusion.69, bf16[256,16,128]{0,2,1:T(8,128)(2,1)S(1)} %bitcast.190, f32[256,16]{0,1:T(8,128)S(1)} %get-tuple-element.404), kind=kOutput, calls=%fused_computation.21 | convolution fusion | flops 137887744 | bytes 8404992 | tf_op jit(solution)/shard_map/while/body/eval_jaxpr/she,hef->shf/dot_general | solution.py:53
  324.1 1.4 copy.167
  (59 shorter events, 0.5 us)
Async XLA Ops:
  7.2 3.5 %copy-start = (bf16[256,2048]{1,0:T(8,128)(2,1)S(1)}, bf16[256,2048]{1,0:T(8,128)(2,1)}, u32[]{:S(2)}) copy-start(bf16[256,2048]{1,0:T(8,128)(2,1)} %param.14) | copy-start | bytes 3145732
  7.2 133.2 %all-gather.6.cloned.1.call-start = ((), (), s32[]{:S(2)}) async-start(), calls=%async_computation | async-start | bytes 9437184 | tf_op jit(solution)/shard_map/all_gather | solution.py:15
  10.7 25.8 %copy-start.3 = (bf16[256,2048]{0,1:T(8,128)(2,1)}, bf16[256,2048]{0,1:T(8,128)(2,1)S(1)}, u32[]{:S(2)}) copy-start(bf16[256,2048]{0,1:T(8,128)(2,1)S(1)} %copy.131) | copy-start | bytes 3145732
  12.6 289.0 %all-gather.8.cloned.1.call-start = ((), (), s32[]{:S(2)}) async-start(), calls=%async_computation.1 | async-start | bytes 9437184 | tf_op jit(solution)/shard_map/all_gather | solution.py:15
  38.0 1.3 copy-start.8
  39.3 101.1 %copy-start.6 = (f32[16,128,128]{2,1,0:T(8,128)S(1)}, f32[16,128,128]{2,1,0:T(8,128)}, u32[]{:S(2)}) copy-start(f32[16,128,128]{2,1,0:T(8,128)} %custom-call.1) | copy-start | bytes 3145732
  154.0 1.0 copy-start.12
  154.0 1.0 copy-start.14
  154.5 1.6 copy-start.7
  158.3 3.0 copy-start.15
  158.3 3.0 copy-start.16
  176.7 1.9 copy-start.1
  178.6 1.9 copy-start.2
  178.7 1.9 copy-start.13
  181.0 1.6 copy-start.4
  182.6 1.3 copy-start.9
  187.9 3.9 %copy-start.10 = (bf16[16,256,256]{2,1,0:T(8,128)(2,1)S(1)}, bf16[16,256,256]{2,1,0:T(8,128)(2,1)}, u32[]{:S(2)}) copy-start(bf16[16,256,256]{2,1,0:T(8,128)(2,1)} %copy-done.9) | copy-start | bytes 6291460
  301.7 12.1 %copy-start.5 = (bf16[256,2048]{0,1:T(8,128)(2,1)S(1)}, bf16[256,2048]{0,1:T(8,128)(2,1)}, u32[]{:S(2)}) copy-start(bf16[256,2048]{0,1:T(8,128)(2,1)} %copy-done.3) | copy-start | bytes 3145732
  316.5 1.9 copy-start.11
Sparse Core Ops, SparseCore 0:
  12.7 127.6 all-gather.5
  178.8 122.8 all-gather.7
where the time goes:
time: 333 us; the launch traced here: 332 us
  waiting for transfers between devices  207 us (62%)
  other arithmetic  33.6 us (10%)
  matrix products  31.4 us (9%)
  blocking collectives  28.6 us (9%)
  local copies, waits for them, and re-layouts  16.8 us (5%)
  between operations  14.4 us (4%)
    all_gather x2, waiting for transfers between devices, prefix(): everything = jax.tree.map(lambda part: lax.all_gather(part, axis), shard)  207 us
    select_n x16, other arithmetic, lap(): return jax.tree.map(lambda a, b: jnp.where(reached, a, b), new, before)  23.5 us
    all_gather x1, blocking collectives, prefix(): everything = jax.tree.map(lambda part: lax.all_gather(part, axis), shard)  22.2 us
    dot_general x8, matrix products, state_product(): jnp.einsum(form, left, upper, preferred_element_type=jnp.float32)  11.1 us
    unnamed x39, local copies, waits for them, and re-layouts  11.1 us
  transfers between devices with their start and end apart: 2, of which 2 were waited for; matrix products, arithmetic and copies ran while one was open for 6% of the time, Pallas kernels for 0%

commit v1 on v0

v1 whole, which is shorter than its diff:
```python
import functools

import jax
import jax.numpy as jnp
from jax import lax
from jax.experimental import pallas as pl
from jax.experimental.pallas import tpu as pltpu
from jax.sharding import PartitionSpec as P

BLK = 256
D = 8192
HD = 128
epsilon = 1e-06
MESH = pl.DeviceIdType.MESH
F32 = jnp.float32
BF16 = jnp.bfloat16


def dot(a, b, ca, cb):
    return lax.dot_general(a, b, (((ca,), (cb,)), ((), ())), preferred_element_type=F32)


def kernel(
    n_seq, n_head, heads,
    q_hbm, k_hbm, v_hbm, ld_ref, gate_hbm, gain_ref, prior_hbm, og_hbm,
    att_hbm, gq_hbm, gk_hbm, gv_hbm, gg_hbm,
    q, k, v, gate, og, prior,
    att, gq, gk, gv, gg,
    run_col, run_row, dec, dec_x,
    own, cross, enter, part, pass_z, pass_x, used,
    own_b, cross_b, enter_b, part_b, pass_z_b, pass_x_b,
    wts, mix, ctx, gnorm, grad, gk_acc, gv_acc,
    sq_acc, rd_acc, sums, sums_in,
    in_sem, out_sem, dec_send, dec_recv, sum_send, sum_recv,
    s_send, s_recv, z_send, z_recv, x_send, x_recv,
    bs_send, bs_recv, bz_send, bz_recv, bx_send, bx_recv,
):
    half = heads // 2
    me = lax.axis_index("seq")
    row = lax.axis_index("head")
    pair, side = me // 2, me % 2
    last = n_seq // 2 - 1
    partner = me + 1 - 2 * side
    mine, theirs = side * half, (1 - side) * half

    barrier = pltpu.get_barrier_semaphore()

    def greet(**target):
        pl.semaphore_signal(barrier, inc=1, device_id=target, device_id_type=MESH)

    greet(seq=partner)
    for d in range(1, n_head):
        greet(head=lax.rem(row + d, n_head))

    @pl.when(pair > 0)
    def _():
        greet(seq=me - 2)

    @pl.when(pair < last)
    def _():
        greet(seq=me + 2)

    loads = [
        pltpu.make_async_copy(src, dst, in_sem.at[j])
        for j, (src, dst) in enumerate(
            [(k_hbm, k), (v_hbm, v), (q_hbm, q), (gate_hbm, gate), (og_hbm, og), (prior_hbm, prior)]
        )
    ]
    for load in loads:
        load.start()

    ti = lax.broadcasted_iota(jnp.int32, (BLK, BLK), 0)
    si = lax.broadcasted_iota(jnp.int32, (BLK, BLK), 1)
    causal = ti >= si
    low = jnp.where(causal, 1.0, 0.0).astype(F32)
    ld = ld_ref[...]
    col = lax.dot_general(
        low, ld, (((1,), (0,)), ((), ())), precision=lax.Precision.HIGHEST, preferred_element_type=F32
    )
    run_row[...] = lax.dot_general(
        ld, low, (((0,), (1,)), ((), ())), precision=lax.Precision.HIGHEST, preferred_element_type=F32
    )
    for h in range(heads):
        wide = jnp.broadcast_to(col[:, h : h + 1], (BLK, HD))
        run_col[h] = wide
        dec[h : h + 1, :] = jnp.exp(wide[BLK - 1 : BLK, :])

    def cols(h):
        return pl.ds(pl.multiple_of(h * HD, HD), HD)

    def send(src, dst, s, r, **target):
        return pltpu.make_async_remote_copy(
            src_ref=src, dst_ref=dst, send_sem=s, recv_sem=r, device_id=target, device_id_type=MESH
        )

    sum_copies = [
        send(sums, sums_in.at[d - 1], sum_send.at[d - 1], sum_recv.at[d - 1], head=lax.rem(row + d, n_head))
        for d in range(1, n_head)
    ]
    dec_copy = send(dec, dec_x, dec_send, dec_recv, seq=partner)

    def s_copy(i):
        return send(own.at[theirs + i], cross.at[i], s_send.at[i], s_recv.at[i], seq=partner)

    def z_copy(i):
        return send(pass_z.at[i], enter.at[i], z_send.at[i], z_recv.at[i], seq=me + 2)

    def x_copy(i):
        return send(pass_x.at[i], part.at[i], x_send.at[i], x_recv.at[i], seq=partner)

    def bs_copy(i):
        return send(own_b.at[theirs + i], cross_b.at[i], bs_send.at[i], bs_recv.at[i], seq=partner)

    def bz_copy(i):
        return send(pass_z_b.at[i], enter_b.at[i], bz_send.at[i], bz_recv.at[i], seq=me - 2)

    def bx_copy(i):
        return send(pass_x_b.at[i], part_b.at[i], bx_send.at[i], bx_recv.at[i], seq=partner)

    def remain_of(h):
        wide = run_col[h]
        return jnp.exp(wide[BLK - 1 : BLK, :] - wide)

    def summary(h):
        scaled = (k[:, cols(h)].astype(F32) * remain_of(h)).astype(BF16)
        own[h] = dot(scaled, v[:, cols(h)], 0, 0)

    loads[0].wait()
    loads[1].wait()
    pl.semaphore_wait(
        barrier, n_head + jnp.where(pair > 0, 1, 0) + jnp.where(pair < last, 1, 0)
    )
    dec_copy.start()

    @pl.loop(0, half)
    def _(i):
        summary(theirs + i)
        s_copy(i).start()

    for load in loads[2:]:
        load.wait()
    dec_copy.wait_recv()
    sq_acc[...] = jnp.zeros_like(sq_acc)
    rd_acc[...] = jnp.zeros_like(rd_acc)

    def within(h):
        spread = jnp.broadcast_to(run_col[h][:, :1], (BLK, BLK)) - run_row[pl.ds(h, 1), :]
        w = jnp.where(causal, jnp.exp(jnp.minimum(spread, 0.0)), 0.0)
        wts[h] = w
        m = (dot(q[:, cols(h)], k[:, cols(h)], 1, 1) * w).astype(BF16)
        mix[h] = m
        ctx[h] = dot(m, v[:, cols(h)], 1, 0)
        opened = jax.nn.sigmoid(gate[:, cols(h)].astype(F32))
        gnorm[h] = og[:, cols(h)].astype(F32) * gain_ref[:, cols(h)] * opened

    def finish(h, state):
        c = ctx[h] + jnp.exp(run_col[h]) * dot(q[:, cols(h)], state.astype(BF16), 1, 0)
        ctx[h] = c
        sq_acc[...] += c * c
        rd_acc[...] += c * gnorm[h]

    first = side == 0

    @pl.loop(0, half)
    def _(i):
        h = mine + i
        summary(h)
        within(h)
        within(theirs + i)

        @pl.when(pair == 0)
        def _():
            enter[i] = prior[h]

        @pl.when(pair > 0)
        def _():
            z_copy(i).wait_recv()

        s_copy(i).wait_recv()
        came = enter[i]
        a, b = own[h], cross[i]
        da, db = dec[pl.ds(h, 1), :], dec_x[pl.ds(h, 1), :]
        mid = jnp.where(first, da, db) * came + jnp.where(first, a, b)
        pass_z[i] = jnp.where(first, db, da) * mid + jnp.where(first, b, a)

        @pl.when(pair < last)
        def _():
            z_copy(i).start()

        pass_x[i] = jnp.where(first, mid, came)
        x_copy(i).start()
        state = jnp.where(first, came, mid)
        used[h] = state
        finish(h, state)

    @pl.loop(0, half)
    def _(i):
        x_copy(i).wait_recv()
        state = part[i]
        used[theirs + i] = state
        finish(theirs + i, state)

    sums[...] = jnp.zeros_like(sums)
    sums[0:1, :] = jnp.sum(sq_acc[...].T, axis=0, keepdims=True)
    sums[1:2, :] = jnp.sum(rd_acc[...].T, axis=0, keepdims=True)
    for copy in sum_copies:
        copy.start()
    total = sums[...]
    for d, copy in enumerate(sum_copies):
        copy.wait_recv()
        total = total + sums_in[d]
    inv_row = lax.rsqrt(total[0:1, :] / D + epsilon)
    coef_row = inv_row * inv_row * inv_row * total[1:2, :] / D
    sq_acc[...] = jnp.broadcast_to(inv_row, (HD, BLK)).T
    rd_acc[...] = jnp.broadcast_to(coef_row, (HD, BLK)).T

    def gradient(h):
        g = (sq_acc[...] * gnorm[h] - ctx[h] * rd_acc[...]).astype(BF16)
        grad[h] = g
        scaled = (q[:, cols(h)].astype(F32) * jnp.exp(run_col[h])).astype(BF16)
        own_b[h] = dot(scaled, g, 0, 0)

    @pl.loop(0, half)
    def _(i):
        gradient(theirs + i)
        bs_copy(i).start()

    def local_back(h):
        g, w = grad[h], wts[h]
        gm = (dot(g, v[:, cols(h)], 1, 1) * w).astype(BF16)
        gq[:, cols(h)] = (
            dot(gm, k[:, cols(h)], 1, 0) + jnp.exp(run_col[h]) * dot(g, used[h].astype(BF16), 1, 1)
        ).astype(BF16)
        gk_acc[h] = dot(gm, q[:, cols(h)], 0, 0)
        gv_acc[h] = dot(mix[h], g, 0, 0)
        normed = ctx[h] * sq_acc[...]
        opened = jax.nn.sigmoid(gate[:, cols(h)].astype(F32))
        att[:, cols(h)] = (normed * gain_ref[:, cols(h)] * opened).astype(BF16)
        gg[:, cols(h)] = (gnorm[h] * normed * (1.0 - opened)).astype(BF16)

    def finish_back(h, state):
        remain = remain_of(h)
        s = state.astype(BF16)
        gk[:, cols(h)] = (gk_acc[h] + remain * dot(v[:, cols(h)], s, 1, 1)).astype(BF16)
        gv[:, cols(h)] = (gv_acc[h] + remain * dot(k[:, cols(h)], s, 1, 0)).astype(BF16)

    @pl.loop(0, half)
    def _(i):
        h = mine + i
        gradient(h)
        local_back(h)
        local_back(theirs + i)

        @pl.when(pair == last)
        def _():
            enter_b[i] = jnp.zeros((HD, HD), F32)

        @pl.when(pair < last)
        def _():
            bz_copy(i).wait_recv()

        bs_copy(i).wait_recv()
        came = enter_b[i]
        a, b = own_b[h], cross_b[i]
        da, db = dec[pl.ds(h, 1), :], dec_x[pl.ds(h, 1), :]
        mid = jnp.where(first, db, da) * came + jnp.where(first, b, a)
        pass_z_b[i] = jnp.where(first, da, db) * mid + jnp.where(first, a, b)

        @pl.when(pair > 0)
        def _():
            bz_copy(i).start()

        pass_x_b[i] = jnp.where(first, came, mid)
        bx_copy(i).start()
        finish_back(h, jnp.where(first, mid, came))

    stores = [
        pltpu.make_async_copy(src, dst, out_sem.at[j])
        for j, (src, dst) in enumerate(
            [(att, att_hbm), (gq, gq_hbm), (gg, gg_hbm), (gk, gk_hbm), (gv, gv_hbm)]
        )
    ]
    for store in stores[:3]:
        store.start()

    @pl.loop(0, half)
    def _(i):
        bx_copy(i).wait_recv()
        finish_back(theirs + i, part_b[i])

    for store in stores[3:]:
        store.start()

    dec_copy.wait_send()
    for copy in sum_copies:
        copy.wait_send()

    @pl.loop(0, half)
    def _(i):
        s_copy(i).wait_send()
        x_copy(i).wait_send()
        bs_copy(i).wait_send()
        bx_copy(i).wait_send()

        @pl.when(pair < last)
        def _():
            z_copy(i).wait_send()

        @pl.when(pair > 0)
        def _():
            bz_copy(i).wait_send()

    for store in stores:
        store.wait()


def solution(mesh):
    n_seq, n_head = mesh.shape["seq"], mesh.shape["head"]

    def shards(queries, key_rows, value_rows, log_decay, gate_input, out_gain, prior_state, out_grad):
        length, features = queries.shape
        heads = log_decay.shape[1]
        half = heads // 2
        wide = (length, features)
        anywhere = pl.BlockSpec(memory_space=pl.ANY)
        vmem = pl.BlockSpec(memory_space=pltpu.VMEM)

        def states(count):
            return pltpu.VMEM((count, HD, HD), F32)

        dma = pltpu.SemaphoreType.DMA
        return pl.pallas_call(
            functools.partial(kernel, n_seq, n_head, heads),
            out_shape=[jax.ShapeDtypeStruct(wide, BF16)] * 5,
            in_specs=[anywhere, anywhere, anywhere, vmem, anywhere, vmem, anywhere, anywhere],
            out_specs=[anywhere] * 5,
            scratch_shapes=[pltpu.VMEM(wide, BF16)] * 5
            + [states(heads)]
            + [pltpu.VMEM(wide, BF16)] * 5
            + [
                pltpu.VMEM((heads, BLK, HD), F32),
                pltpu.VMEM((heads, BLK), F32),
                pltpu.VMEM((heads, HD), F32),
                pltpu.VMEM((heads, HD), F32),
            ]
            + [states(heads)] + [states(half)] * 5 + [states(heads)]
            + [states(heads)] + [states(half)] * 5
            + [
                pltpu.VMEM((heads, BLK, BLK), F32),
                pltpu.VMEM((heads, BLK, BLK), BF16),
                pltpu.VMEM((heads, BLK, HD), F32),
                pltpu.VMEM((heads, BLK, HD), F32),
                pltpu.VMEM((heads, BLK, HD), BF16),
                pltpu.VMEM((heads, BLK, HD), F32),
                pltpu.VMEM((heads, BLK, HD), F32),
                pltpu.VMEM((BLK, HD), F32),
                pltpu.VMEM((BLK, HD), F32),
                pltpu.VMEM((8, BLK), F32),
                pltpu.VMEM((n_head - 1, 8, BLK), F32),
                dma((6,)),
                dma((5,)),
                dma,
                dma,
                dma((n_head - 1,)),
                dma((n_head - 1,)),
            ]
            + [dma((half,))] * 12,
            compiler_params=pltpu.CompilerParams(
                collective_id=0, has_side_effects=True, vmem_limit_bytes=56 * 1024 * 1024
            ),
            cost_estimate=pl.CostEstimate(
                flops=4_000_000_000, bytes_accessed=12_000_000, transcendentals=2_000_000
            ),
        )(
            queries, key_rows, value_rows, log_decay, gate_input,
            out_gain.reshape(1, features), prior_state, out_grad,
        )

    cut = P("seq", "head")
    return jax.shard_map(
        shards,
        mesh=mesh,
        in_specs=(cut, cut, cut, cut, cut, P("head"), P("head", None, None), cut),
        out_specs=(cut,) * 5,
        check_vma=False,
    )
```

time: 333 us -> 75.7 us (0.23)
  waiting for transfers between devices: 207 us -> 0 us
  Pallas kernels: 0 us -> 65 us
  other arithmetic: 33.6 us -> 0 us
  matrix products: 31.4 us -> 0 us
  blocking collectives: 28.6 us -> 0 us
  between operations: 14.4 us -> 0.65 us
  local copies, waits for them, and re-layouts: 16.8 us -> 9.65 us
    all_gather x2 -> x0, waiting for transfers between devices: 207 us -> none  [prefix(): everything = jax.tree.map(lambda part: lax.all_gather(part, axis), shard)]
    pallas_call x0 -> x1, Pallas kernels: none -> 65 us  [shards(): pl.pallas_call(functools.partial(kernel, n_seq, n_head, heads), out_shape...]
    dot_general x22 -> x0, matrix products: 31.4 us -> none  [the longest x8 11.1 us: state_product(): jnp.einsum(form, left, upper, preferred_element_type=jnp.float32)]
    select_n x16 -> x0, other arithmetic: 23.5 us -> none  [lap(): return jax.tree.map(lambda a, b: jnp.where(reached, a, b), new, before)]
    all_gather x1 -> x0, blocking collectives: 22.2 us -> none  [prefix(): everything = jax.tree.map(lambda part: lax.all_gather(part, axis), shard)]
    convert_element_type x2 -> x0, other arithmetic: 6.55 us -> none  [the longest x1 4.98 us: shards(): (grad_wide * normed * out_gain * opened * (1.0 - opened)).astype(jnp.bflo...]
    psum x1 -> x0, blocking collectives: 6.34 us -> none  [shards(): squares = lax.psum(jnp.sum(merged * merged, axis=1), 'head')]
    reshape x2 -> x0, local copies, waits for them, and re-layouts: 3.79 us -> none  [the longest x1 3 us: shards(): merged = context.reshape(length, features)]
  transfers between devices with their start and end apart: 2 -> 0, of which waited for: 2 -> 0; matrix products, arithmetic and copies ran while one was open for 6% -> 0% of each run, Pallas kernels for 0% -> 0%
where the time goes in v1:
time: 75.7 us; the launch traced here: 75.3 us
  Pallas kernels  65 us (86%)
  local copies, waits for them, and re-layouts  9.65 us (13%)
    pallas_call x1, Pallas kernels, shards(): pl.pallas_call(functools.partial(kernel, n_seq, n_head, heads), out_shape...  65 us
    unnamed x14, local copies, waits for them, and re-layouts  9.65 us

profile of v1, /device:TPU:0, one launch (start us, length us, event | category | flops | bytes accessed | tf_op | source)
XLA Modules:
  0.0 75.3 jit_solution(11673444951016926489)
XLA Ops:
  0.6 1.5 %copy.13.ld_ref = f32[256,16]{1,0:T(8,128)} copy(f32[256,16]{0,1:T(8,128)} %param.11) | data formatting | bytes 32768 | tf_op args[3]
  2.1 65.0 %shard_map.119 = (bf16[256,2048]{1,0:T(8,128)(2,1)}, bf16[256,2048]{1,0:T(8,128)(2,1)}, bf16[256,2048]{1,0:T(8,128)(2,1)}, bf16[256,2048]{1,0:T(8,128)(2,1)}, bf16[256,2048]{1,0:T(8,128)(2,1)}) custom-call(bf16[256,2048]{1,0:T(8,128)(2,1)} %q_hbm.1, bf16[256,2048]{1,0:T(8,128)(2,1)} %k_hbm.1, bf16[256,2048]{1,0:T(8,128)(2,1)} %v_hbm.1, ...), custom_call_target="tpu_custom_call" | custom-call | flops 4000000000 | bytes 12000000 | tf_op jit(solution)/shard_map/pallas_call | solution.py:332
  67.1 0.0 copy-start.3
  67.2 2.4 %copy.19 = bf16[256,2048]{1,0:T(8,128)(2,1)} copy(bf16[256,2048]{1,0:T(8,128)(2,1)} %get-tuple-element.10) | data formatting | bytes 2097152
  69.5 0.0 copy-done.3
  69.6 0.0 copy-start.2
  69.6 1.0 %copy.20 = bf16[256,2048]{1,0:T(8,128)(2,1)} copy(bf16[256,2048]{1,0:T(8,128)(2,1)S(1)} %copy-done.3) | data formatting | bytes 2097152
  70.5 0.6 copy-done.2
  71.2 0.0 copy-start.1
  71.2 1.0 %copy.21 = bf16[256,2048]{1,0:T(8,128)(2,1)} copy(bf16[256,2048]{1,0:T(8,128)(2,1)S(1)} %copy-done.2) | data formatting | bytes 2097152
  72.1 0.6 copy-done.1
  72.8 0.0 copy-start
  72.8 1.0 %copy.22 = bf16[256,2048]{1,0:T(8,128)(2,1)} copy(bf16[256,2048]{1,0:T(8,128)(2,1)S(1)} %copy-done.1) | data formatting | bytes 2097152
  73.7 0.6 copy-done
  74.4 1.0 %copy.23 = bf16[256,2048]{1,0:T(8,128)(2,1)} copy(bf16[256,2048]{1,0:T(8,128)(2,1)S(1)} %copy-done) | data formatting | bytes 2097152
Async XLA Ops:
  67.1 2.4 %copy-start.3 = (bf16[256,2048]{1,0:T(8,128)(2,1)S(1)}, bf16[256,2048]{1,0:T(8,128)(2,1)}, u32[]{:S(2)}) copy-start(bf16[256,2048]{1,0:T(8,128)(2,1)} %get-tuple-element.11) | copy-start | bytes 3145732
  69.6 1.6 %copy-start.2 = (bf16[256,2048]{1,0:T(8,128)(2,1)S(1)}, bf16[256,2048]{1,0:T(8,128)(2,1)}, u32[]{:S(2)}) copy-start(bf16[256,2048]{1,0:T(8,128)(2,1)} %get-tuple-element.12) | copy-start | bytes 3145732
  71.2 1.6 %copy-start.1 = (bf16[256,2048]{1,0:T(8,128)(2,1)S(1)}, bf16[256,2048]{1,0:T(8,128)(2,1)}, u32[]{:S(2)}) copy-start(bf16[256,2048]{1,0:T(8,128)(2,1)} %get-tuple-element.13) | copy-start | bytes 3145732
  72.8 1.6 %copy-start = (bf16[256,2048]{1,0:T(8,128)(2,1)S(1)}, bf16[256,2048]{1,0:T(8,128)(2,1)}, u32[]{:S(2)}) copy-start(bf16[256,2048]{1,0:T(8,128)(2,1)} %get-tuple-element.14) | copy-start | bytes 3145732

commit v2 on v1

--- a/solution.py
+++ b/solution.py
@@ -10,6 +10,9 @@
 BLK = 256
 D = 8192
 HD = 128
+PARTS = 2
+LAG = 2
+ROWS = HD // PARTS
 epsilon = 1e-06
 MESH = pl.DeviceIdType.MESH
 F32 = jnp.float32
@@ -28,7 +31,7 @@
     att, gq, gk, gv, gg,
     run_col, run_row, dec, dec_x,
     own, cross, enter, part, pass_z, pass_x, used,
-    own_b, cross_b, enter_b, part_b, pass_z_b, pass_x_b,
+    own_b, cross_b, enter_b, part_b, pass_z_b, pass_x_b, used_b,
     wts, mix, ctx, gnorm, grad, gk_acc, gv_acc,
     sq_acc, rd_acc, sums, sums_in,
     in_sem, out_sem, dec_send, dec_recv, sum_send, sum_recv,
@@ -75,10 +78,10 @@
     low = jnp.where(causal, 1.0, 0.0).astype(F32)
     ld = ld_ref[...]
     col = lax.dot_general(
-        low, ld, (((1,), (0,)), ((), ())), precision=lax.Precision.HIGHEST, preferred_element_type=F32
+        low, ld, (((1,), (1,)), ((), ())), precision=lax.Precision.HIGHEST, preferred_element_type=F32
     )
     run_row[...] = lax.dot_general(
-        ld, low, (((0,), (1,)), ((), ())), precision=lax.Precision.HIGHEST, preferred_element_type=F32
+        ld, low, (((1,), (1,)), ((), ())), precision=lax.Precision.HIGHEST, preferred_element_type=F32
     )
     for h in range(heads):
         wide = jnp.broadcast_to(col[:, h : h + 1], (BLK, HD))
@@ -99,23 +102,32 @@
     ]
     dec_copy = send(dec, dec_x, dec_send, dec_recv, seq=partner)
 
-    def s_copy(i):
-        return send(own.at[theirs + i], cross.at[i], s_send.at[i], s_recv.at[i], seq=partner)
-
-    def z_copy(i):
-        return send(pass_z.at[i], enter.at[i], z_send.at[i], z_recv.at[i], seq=me + 2)
-
-    def x_copy(i):
-        return send(pass_x.at[i], part.at[i], x_send.at[i], x_recv.at[i], seq=partner)
-
-    def bs_copy(i):
-        return send(own_b.at[theirs + i], cross_b.at[i], bs_send.at[i], bs_recv.at[i], seq=partner)
-
-    def bz_copy(i):
-        return send(pass_z_b.at[i], enter_b.at[i], bz_send.at[i], bz_recv.at[i], seq=me - 2)
-
-    def bx_copy(i):
-        return send(pass_x_b.at[i], part_b.at[i], bx_send.at[i], bx_recv.at[i], seq=partner)
+    def piece(ref, i, j):
+        return ref.at[i, pl.ds(j * ROWS, ROWS)]
+
+    def s_copy(i, j):
+        n = i * PARTS + j
+        return send(piece(own, theirs + i, j), piece(cross, i, j), s_send.at[n], s_recv.at[n], seq=partner)
+
+    def z_copy(i, j):
+        n = i * PARTS + j
+        return send(piece(pass_z, i, j), piece(enter, i, j), z_send.at[n], z_recv.at[n], seq=me + 2)
+
+    def x_copy(i, j):
+        n = i * PARTS + j
+        return send(piece(pass_x, i, j), piece(part, i, j), x_send.at[n], x_recv.at[n], seq=partner)
+
+    def bs_copy(i, j):
+        n = i * PARTS + j
+        return send(piece(own_b, theirs + i, j), piece(cross_b, i, j), bs_send.at[n], bs_recv.at[n], seq=partner)
+
+    def bz_copy(i, j):
+        n = i * PARTS + j
+        return send(piece(pass_z_b, i, j), piece(enter_b, i, j), bz_send.at[n], bz_recv.at[n], seq=me - 2)
+
+    def bx_copy(i, j):
+        n = i * PARTS + j
+        return send(piece(pass_x_b, i, j), piece(part_b, i, j), bx_send.at[n], bx_recv.at[n], seq=partner)
 
     def remain_of(h):
         wide = run_col[h]
@@ -135,7 +147,8 @@
     @pl.loop(0, half)
     def _(i):
         summary(theirs + i)
-        s_copy(i).start()
+        for j in range(PARTS):
+            s_copy(i, j).start()
 
     for load in loads[2:]:
         load.wait()
@@ -161,44 +174,68 @@
 
     first = side == 0
 
-    @pl.loop(0, half)
-    def _(i):
+    def chain(i):
         h = mine + i
-        summary(h)
-        within(h)
-        within(theirs + i)
-
-        @pl.when(pair == 0)
-        def _():
-            enter[i] = prior[h]
-
-        @pl.when(pair > 0)
-        def _():
-            z_copy(i).wait_recv()
-
-        s_copy(i).wait_recv()
-        came = enter[i]
-        a, b = own[h], cross[i]
         da, db = dec[pl.ds(h, 1), :], dec_x[pl.ds(h, 1), :]
-        mid = jnp.where(first, da, db) * came + jnp.where(first, a, b)
-        pass_z[i] = jnp.where(first, db, da) * mid + jnp.where(first, b, a)
-
-        @pl.when(pair < last)
-        def _():
-            z_copy(i).start()
-
-        pass_x[i] = jnp.where(first, mid, came)
-        x_copy(i).start()
-        state = jnp.where(first, came, mid)
-        used[h] = state
-        finish(h, state)
-
-    @pl.loop(0, half)
-    def _(i):
-        x_copy(i).wait_recv()
-        state = part[i]
-        used[theirs + i] = state
-        finish(theirs + i, state)
+        d0, d1 = jnp.where(first, da, db), jnp.where(first, db, da)
+        for j in range(PARTS):
+            rows = pl.ds(j * ROWS, ROWS)
+            s_copy(i, j).wait_recv()
+
+            @pl.when(pair == 0)
+            def _():
+                enter[i, rows] = prior[h, rows]
+
+            @pl.when(pair > 0)
+            def _():
+                z_copy(i, j).wait_recv()
+
+            came = enter[i, rows]
+            a, b = own[h, rows], cross[i, rows]
+            mid = d0 * came + jnp.where(first, a, b)
+            pass_z[i, rows] = d1 * mid + jnp.where(first, b, a)
+
+            @pl.when(pair < last)
+            def _():
+                z_copy(i, j).start()
+
+            pass_x[i, rows] = jnp.where(first, mid, came)
+            x_copy(i, j).start()
+            used[h, rows] = jnp.where(first, came, mid)
+
+    def receive(i):
+        for j in range(PARTS):
+            x_copy(i, j).wait_recv()
+        used[theirs + i] = part[i]
+        finish(theirs + i, part[i])
+
+    @pl.loop(0, half + last + LAG)
+    def _(t):
+        step = t - pair
+        active = jnp.logical_and(step >= 0, step < half)
+
+        @pl.when(t < half)
+        def _():
+            summary(mine + t)
+
+        @pl.when(active)
+        def _():
+            chain(step)
+
+        @pl.when(t < half)
+        def _():
+            within(mine + t)
+            within(theirs + t)
+
+        @pl.when(active)
+        def _():
+            finish(mine + step, used[mine + step])
+
+        late = step - LAG
+
+        @pl.when(jnp.logical_and(late >= 0, late < half))
+        def _():
+            receive(late)
 
     sums[...] = jnp.zeros_like(sums)
     sums[0:1, :] = jnp.sum(sq_acc[...].T, axis=0, keepdims=True)
@@ -223,7 +260,8 @@
     @pl.loop(0, half)
     def _(i):
         gradient(theirs + i)
-        bs_copy(i).start()
+        for j in range(PARTS):
+            bs_copy(i, j).start()
 
     def local_back(h):
         g, w = grad[h], wts[h]
@@ -244,35 +282,64 @@
         gk[:, cols(h)] = (gk_acc[h] + remain * dot(v[:, cols(h)], s, 1, 1)).astype(BF16)
         gv[:, cols(h)] = (gv_acc[h] + remain * dot(k[:, cols(h)], s, 1, 0)).astype(BF16)
 
-    @pl.loop(0, half)
-    def _(i):
+    def chain_back(i):
         h = mine + i
-        gradient(h)
-        local_back(h)
-        local_back(theirs + i)
-
-        @pl.when(pair == last)
-        def _():
-            enter_b[i] = jnp.zeros((HD, HD), F32)
-
-        @pl.when(pair < last)
-        def _():
-            bz_copy(i).wait_recv()
-
-        bs_copy(i).wait_recv()
-        came = enter_b[i]
-        a, b = own_b[h], cross_b[i]
         da, db = dec[pl.ds(h, 1), :], dec_x[pl.ds(h, 1), :]
-        mid = jnp.where(first, db, da) * came + jnp.where(first, b, a)
-        pass_z_b[i] = jnp.where(first, da, db) * mid + jnp.where(first, a, b)
-
-        @pl.when(pair > 0)
-        def _():
-            bz_copy(i).start()
-
-        pass_x_b[i] = jnp.where(first, came, mid)
-        bx_copy(i).start()
-        finish_back(h, jnp.where(first, mid, came))
+        d0, d1 = jnp.where(first, da, db), jnp.where(first, db, da)
+        for j in range(PARTS):
+            rows = pl.ds(j * ROWS, ROWS)
+            bs_copy(i, j).wait_recv()
+
+            @pl.when(pair == last)
+            def _():
+                enter_b[i, rows] = jnp.zeros((ROWS, HD), F32)
+
+            @pl.when(pair < last)
+            def _():
+                bz_copy(i, j).wait_recv()
+
+            came = enter_b[i, rows]
+            a, b = own_b[h, rows], cross_b[i, rows]
+            mid = d1 * came + jnp.where(first, b, a)
+            pass_z_b[i, rows] = d0 * mid + jnp.where(first, a, b)
+
+            @pl.when(pair > 0)
+            def _():
+                bz_copy(i, j).start()
+
+            pass_x_b[i, rows] = jnp.where(first, came, mid)
+            bx_copy(i, j).start()
+            used_b[i, rows] = jnp.where(first, mid, came)
+
+    @pl.loop(0, half + last + LAG)
+    def _(t):
+        step = t - (last - pair)
+        active = jnp.logical_and(step >= 0, step < half)
+
+        @pl.when(t < half)
+        def _():
+            gradient(mine + t)
+
+        @pl.when(active)
+        def _():
+            chain_back(step)
+
+        @pl.when(t < half)
+        def _():
+            local_back(mine + t)
+            local_back(theirs + t)
+
+        @pl.when(active)
+        def _():
+            finish_back(mine + step, used_b[step])
+
+        late = step - LAG
+
+        @pl.when(jnp.logical_and(late >= 0, late < half))
+        def _():
+            for j in range(PARTS):
+                bx_copy(late, j).wait_recv()
+            finish_back(theirs + late, part_b[late])
 
     stores = [
         pltpu.make_async_copy(src, dst, out_sem.at[j])
@@ -280,15 +347,7 @@
             [(att, att_hbm), (gq, gq_hbm), (gg, gg_hbm), (gk, gk_hbm), (gv, gv_hbm)]
         )
     ]
-    for store in stores[:3]:
-        store.start()
-
-    @pl.loop(0, half)
-    def _(i):
-        bx_copy(i).wait_recv()
-        finish_back(theirs + i, part_b[i])
-
-    for store in stores[3:]:
+    for store in stores:
         store.start()
 
     dec_copy.wait_send()
@@ -297,19 +356,37 @@
 
     @pl.loop(0, half)
     def _(i):
-        s_copy(i).wait_send()
-        x_copy(i).wait_send()
-        bs_copy(i).wait_send()
-        bx_copy(i).wait_send()
-
-        @pl.when(pair < last)
-        def _():
-            z_copy(i).wait_send()
-
-        @pl.when(pair > 0)
-        def _():
-            bz_copy(i).wait_send()
-
+        for j in range(PARTS):
+            s_copy(i, j).wait_send()
+            x_copy(i, j).wait_send()
+            bs_copy(i, j).wait_send()
+            bx_copy(i, j).wait_send()
+
+            @pl.when(pair < last)
+            def _():
+                z_copy(i, j).wait_send()
+
+            @pl.when(pair > 0)
+            def _():
+                bz_copy(i, j).wait_send()
+
+    for store in stores:
+        store.wait()
+
+
+def deliver(rows, *refs):
+    sources, targets, staged, (in_sem, out_sem) = refs[:5], refs[5:10], refs[10:15], refs[15:]
+    loads, stores = [], []
+    for j in range(10):
+        part = pl.ds(j // 5 * rows, rows)
+        a, b, c = sources[j % 5].at[part], staged[j % 5].at[part], targets[j % 5].at[part]
+        loads.append(pltpu.make_async_copy(a, b, in_sem.at[j]))
+        stores.append(pltpu.make_async_copy(b, c, out_sem.at[j]))
+    for load in loads:
+        load.start()
+    for load, store in zip(loads, stores):
+        load.wait()
+        store.start()
     for store in stores:
         store.wait()
 
@@ -329,7 +406,7 @@
             return pltpu.VMEM((count, HD, HD), F32)
 
         dma = pltpu.SemaphoreType.DMA
-        return pl.pallas_call(
+        results = pl.pallas_call(
             functools.partial(kernel, n_seq, n_head, heads),
             out_shape=[jax.ShapeDtypeStruct(wide, BF16)] * 5,
             in_specs=[anywhere, anywhere, anywhere, vmem, anywhere, vmem, anywhere, anywhere],
@@ -344,7 +421,7 @@
                 pltpu.VMEM((heads, HD), F32),
             ]
             + [states(heads)] + [states(half)] * 5 + [states(heads)]
-            + [states(heads)] + [states(half)] * 5
+            + [states(heads)] + [states(half)] * 6
             + [
                 pltpu.VMEM((heads, BLK, BLK), F32),
                 pltpu.VMEM((heads, BLK, BLK), BF16),
@@ -364,7 +441,7 @@
                 dma((n_head - 1,)),
                 dma((n_head - 1,)),
             ]
-            + [dma((half,))] * 12,
+            + [dma((half * PARTS,))] * 12,
             compiler_params=pltpu.CompilerParams(
                 collective_id=0, has_side_effects=True, vmem_limit_bytes=56 * 1024 * 1024
             ),
@@ -372,9 +449,18 @@
                 flops=4_000_000_000, bytes_accessed=12_000_000, transcendentals=2_000_000
             ),
         )(
-            queries, key_rows, value_rows, log_decay, gate_input,
+            queries, key_rows, value_rows, log_decay.T, gate_input,
             out_gain.reshape(1, features), prior_state, out_grad,
         )
+        return pl.pallas_call(
+            functools.partial(deliver, length // 2),
+            out_shape=[jax.ShapeDtypeStruct(wide, BF16)] * 5,
+            in_specs=[anywhere] * 5,
+            out_specs=[anywhere] * 5,
+            scratch_shapes=[pltpu.VMEM(wide, BF16)] * 5 + [dma((10,)), dma((10,))],
+            compiler_params=pltpu.CompilerParams(vmem_limit_bytes=60 * 1024 * 1024),
+            cost_estimate=pl.CostEstimate(flops=0, bytes_accessed=10_000_000, transcendentals=0),
+        )(*results)
 
     cut = P("seq", "head")
     return jax.shard_map(

time: 75.7 us -> 86.7 us (1.15)
  Pallas kernels: 65 us -> 85.7 us
  local copies, waits for them, and re-layouts: 9.65 us -> 0 us
    pallas_call x1, Pallas kernels: 65 us -> 81 us  [shards(): pl.pallas_call(functools.partial(kernel, n_seq, n_head, heads), out_shape...]
    unnamed x14 -> x0, local copies, waits for them, and re-layouts: 9.65 us -> none
    pallas_call x0 -> x1, Pallas kernels: none -> 4.71 us  [shards(): pl.pallas_call(functools.partial(deliver, length // 2), out_shape=[jax.Sh...]
where the time goes in v2:
time: 86.7 us; the launch traced here: 86.4 us
  Pallas kernels  85.7 us (99%)
    pallas_call x1, Pallas kernels, shards(): pl.pallas_call(functools.partial(kernel, n_seq, n_head, heads), out_shape...  81 us
    pallas_call x1, Pallas kernels, shards(): pl.pallas_call(functools.partial(deliver, length // 2), out_shape=[jax.Sh...  4.71 us

profile of v2, /device:TPU:0, one launch (start us, length us, event | category | flops | bytes accessed | tf_op | source)
XLA Modules:
  0.0 86.4 jit_solution(7199420852717349435)
XLA Ops:
  0.6 81.0 %shard_map.119 = (bf16[256,2048]{1,0:T(8,128)(2,1)}, bf16[256,2048]{1,0:T(8,128)(2,1)}, bf16[256,2048]{1,0:T(8,128)(2,1)}, bf16[256,2048]{1,0:T(8,128)(2,1)}, bf16[256,2048]{1,0:T(8,128)(2,1)}) custom-call(bf16[256,2048]{1,0:T(8,128)(2,1)} %q_hbm.1, bf16[256,2048]{1,0:T(8,128)(2,1)} %k_hbm.1, bf16[256,2048]{1,0:T(8,128)(2,1)} %v_hbm.1, f32[16,256]{1,0:T(8,128)} %bitcast.2, ...), custom_call_target="tpu_custom_call" | custom-call | flops 4000000000 | bytes 12000000 | tf_op jit(solution)/shard_map/pallas_call | solution.py:409
  81.6 4.7 %shard_map.120 = (bf16[256,2048]{1,0:T(8,128)(2,1)}, bf16[256,2048]{1,0:T(8,128)(2,1)}, bf16[256,2048]{1,0:T(8,128)(2,1)}, bf16[256,2048]{1,0:T(8,128)(2,1)}, bf16[256,2048]{1,0:T(8,128)(2,1)}) custom-call(bf16[256,2048]{1,0:T(8,128)(2,1)} %get-tuple-element.10.refs_0_, bf16[256,2048]{1,0:T(8,128)(2,1)} %get-tuple-element.11.refs_1_, ...), custom_call_target="tpu_custom_call" | custom-call | bytes 10000000 | tf_op jit(solution)/shard_map/pallas_call | solution.py:455

commit v3 on v2

--- a/solution.py
+++ b/solution.py
@@ -10,8 +10,9 @@
 BLK = 256
 D = 8192
 HD = 128
-PARTS = 2
-LAG = 2
+PARTS = 1
+LAG = 1
+GROUP = 2
 ROWS = HD // PARTS
 epsilon = 1e-06
 MESH = pl.DeviceIdType.MESH
@@ -26,15 +27,14 @@
 def kernel(
     n_seq, n_head, heads,
     q_hbm, k_hbm, v_hbm, ld_ref, gate_hbm, gain_ref, prior_hbm, og_hbm,
-    att_hbm, gq_hbm, gk_hbm, gv_hbm, gg_hbm,
+    att, gq, gk, gv, gg,
     q, k, v, gate, og, prior,
-    att, gq, gk, gv, gg,
     run_col, run_row, dec, dec_x,
     own, cross, enter, part, pass_z, pass_x, used,
     own_b, cross_b, enter_b, part_b, pass_z_b, pass_x_b, used_b,
     wts, mix, ctx, gnorm, grad, gk_acc, gv_acc,
     sq_acc, rd_acc, sums, sums_in,
-    in_sem, out_sem, dec_send, dec_recv, sum_send, sum_recv,
+    in_sem, dec_send, dec_recv, sum_send, sum_recv,
     s_send, s_recv, z_send, z_recv, x_send, x_recv,
     bs_send, bs_recv, bz_send, bz_recv, bx_send, bx_recv,
 ):
@@ -133,9 +133,11 @@
         wide = run_col[h]
         return jnp.exp(wide[BLK - 1 : BLK, :] - wide)
 
-    def summary(h):
-        scaled = (k[:, cols(h)].astype(F32) * remain_of(h)).astype(BF16)
-        own[h] = dot(scaled, v[:, cols(h)], 0, 0)
+    def summaries(hs):
+        scaled = [(k[:, cols(h)].astype(F32) * remain_of(h)).astype(BF16) for h in hs]
+        made = [dot(a, v[:, cols(h)], 0, 0) for a, h in zip(scaled, hs)]
+        for h, state in zip(hs, made):
+            own[h] = state
 
     loads[0].wait()
     loads[1].wait()
@@ -144,11 +146,21 @@
     )
     dec_copy.start()
 
-    @pl.loop(0, half)
-    def _(i):
-        summary(theirs + i)
-        for j in range(PARTS):
-            s_copy(i, j).start()
+    def spread_of(start, g):
+        return [start + g * GROUP + i for i in range(GROUP)]
+
+    groups = half // GROUP
+
+    @pl.loop(0, groups)
+    def _(g):
+        summaries(spread_of(theirs, g))
+        for i in spread_of(0, g):
+            for j in range(PARTS):
+                s_copy(i, j).start()
+
+    @pl.loop(0, groups)
+    def _(g):
+        summaries(spread_of(mine, g))
 
     for load in loads[2:]:
         load.wait()
@@ -156,21 +168,34 @@
     sq_acc[...] = jnp.zeros_like(sq_acc)
     rd_acc[...] = jnp.zeros_like(rd_acc)
 
-    def within(h):
-        spread = jnp.broadcast_to(run_col[h][:, :1], (BLK, BLK)) - run_row[pl.ds(h, 1), :]
-        w = jnp.where(causal, jnp.exp(jnp.minimum(spread, 0.0)), 0.0)
-        wts[h] = w
-        m = (dot(q[:, cols(h)], k[:, cols(h)], 1, 1) * w).astype(BF16)
-        mix[h] = m
-        ctx[h] = dot(m, v[:, cols(h)], 1, 0)
-        opened = jax.nn.sigmoid(gate[:, cols(h)].astype(F32))
-        gnorm[h] = og[:, cols(h)].astype(F32) * gain_ref[:, cols(h)] * opened
-
-    def finish(h, state):
-        c = ctx[h] + jnp.exp(run_col[h]) * dot(q[:, cols(h)], state.astype(BF16), 1, 0)
-        ctx[h] = c
-        sq_acc[...] += c * c
-        rd_acc[...] += c * gnorm[h]
+    def within(hs):
+        scores = [dot(q[:, cols(h)], k[:, cols(h)], 1, 1) for h in hs]
+        ws = []
+        for h in hs:
+            wide = run_col[h]
+            spread = jnp.concatenate([wide, wide], axis=1) - run_row[pl.ds(h, 1), :]
+            ws.append(jnp.where(causal, jnp.exp(jnp.minimum(spread, 0.0)), 0.0))
+        ms = [(a * w).astype(BF16) for a, w in zip(scores, ws)]
+        rows = [dot(m, v[:, cols(h)], 1, 0) for m, h in zip(ms, hs)]
+        opens = [jax.nn.sigmoid(gate[:, cols(h)].astype(F32)) for h in hs]
+        norms = [og[:, cols(h)].astype(F32) * gain_ref[:, cols(h)] * o for h, o in zip(hs, opens)]
+        for h, w, m, c, o in zip(hs, ws, ms, rows, norms):
+            wts[h] = w
+            mix[h] = m
+            ctx[h] = c
+            gnorm[h] = o
+
+    def finish(hs):
+        across = [dot(q[:, cols(h)], used[h].astype(BF16), 1, 0) for h in hs]
+        cs = [ctx[h] + jnp.exp(run_col[h]) * a for h, a in zip(hs, across)]
+        squares, dots = sq_acc[...], rd_acc[...]
+        for h, c in zip(hs, cs):
+            squares = squares + c * c
+            dots = dots + c * gnorm[h]
+        for h, c in zip(hs, cs):
+            ctx[h] = c
+        sq_acc[...] = squares
+        rd_acc[...] = dots
 
     first = side == 0
 
@@ -203,39 +228,32 @@
             x_copy(i, j).start()
             used[h, rows] = jnp.where(first, came, mid)
 
-    def receive(i):
-        for j in range(PARTS):
-            x_copy(i, j).wait_recv()
-        used[theirs + i] = part[i]
-        finish(theirs + i, part[i])
-
-    @pl.loop(0, half + last + LAG)
+    @pl.loop(0, groups + last + LAG)
     def _(t):
         step = t - pair
-        active = jnp.logical_and(step >= 0, step < half)
-
-        @pl.when(t < half)
-        def _():
-            summary(mine + t)
+        active = jnp.logical_and(step >= 0, step < groups)
+        late = step - LAG
 
         @pl.when(active)
         def _():
-            chain(step)
-
-        @pl.when(t < half)
-        def _():
-            within(mine + t)
-            within(theirs + t)
+            for i in spread_of(0, step):
+                chain(i)
+
+        @pl.when(t < groups)
+        def _():
+            within(spread_of(mine, t) + spread_of(theirs, t))
 
         @pl.when(active)
         def _():
-            finish(mine + step, used[mine + step])
-
-        late = step - LAG
-
-        @pl.when(jnp.logical_and(late >= 0, late < half))
-        def _():
-            receive(late)
+            finish(spread_of(mine, step))
+
+        @pl.when(jnp.logical_and(late >= 0, late < groups))
+        def _():
+            for i in spread_of(0, late):
+                for j in range(PARTS):
+                    x_copy(i, j).wait_recv()
+                used[theirs + i] = part[i]
+            finish(spread_of(theirs, late))
 
     sums[...] = jnp.zeros_like(sums)
     sums[0:1, :] = jnp.sum(sq_acc[...].T, axis=0, keepdims=True)
@@ -251,36 +269,65 @@
     sq_acc[...] = jnp.broadcast_to(inv_row, (HD, BLK)).T
     rd_acc[...] = jnp.broadcast_to(coef_row, (HD, BLK)).T
 
-    def gradient(h):
-        g = (sq_acc[...] * gnorm[h] - ctx[h] * rd_acc[...]).astype(BF16)
-        grad[h] = g
-        scaled = (q[:, cols(h)].astype(F32) * jnp.exp(run_col[h])).astype(BF16)
-        own_b[h] = dot(scaled, g, 0, 0)
-
-    @pl.loop(0, half)
-    def _(i):
-        gradient(theirs + i)
-        for j in range(PARTS):
-            bs_copy(i, j).start()
-
-    def local_back(h):
-        g, w = grad[h], wts[h]
-        gm = (dot(g, v[:, cols(h)], 1, 1) * w).astype(BF16)
-        gq[:, cols(h)] = (
-            dot(gm, k[:, cols(h)], 1, 0) + jnp.exp(run_col[h]) * dot(g, used[h].astype(BF16), 1, 1)
-        ).astype(BF16)
-        gk_acc[h] = dot(gm, q[:, cols(h)], 0, 0)
-        gv_acc[h] = dot(mix[h], g, 0, 0)
-        normed = ctx[h] * sq_acc[...]
-        opened = jax.nn.sigmoid(gate[:, cols(h)].astype(F32))
-        att[:, cols(h)] = (normed * gain_ref[:, cols(h)] * opened).astype(BF16)
-        gg[:, cols(h)] = (gnorm[h] * normed * (1.0 - opened)).astype(BF16)
-
-    def finish_back(h, state):
-        remain = remain_of(h)
-        s = state.astype(BF16)
-        gk[:, cols(h)] = (gk_acc[h] + remain * dot(v[:, cols(h)], s, 1, 1)).astype(BF16)
-        gv[:, cols(h)] = (gv_acc[h] + remain * dot(k[:, cols(h)], s, 1, 0)).astype(BF16)
+    def gradients(hs):
+        inv, coef = sq_acc[...], rd_acc[...]
+        gs = [(inv * gnorm[h] - ctx[h] * coef).astype(BF16) for h in hs]
+        scaled = [(q[:, cols(h)].astype(F32) * jnp.exp(run_col[h])).astype(BF16) for h in hs]
+        made = [dot(a, g, 0, 0) for a, g in zip(scaled, gs)]
+        for h, g, state in zip(hs, gs, made):
+            grad[h] = g
+            own_b[h] = state
+
+    @pl.loop(0, groups)
+    def _(g):
+        gradients(spread_of(theirs, g))
+        for i in spread_of(0, g):
+            for j in range(PARTS):
+                bs_copy(i, j).start()
+
+    @pl.loop(0, groups)
+    def _(g):
+        gradients(spread_of(mine, g))
+
+    def local_back(hs):
+        gs = [grad[h] for h in hs]
+        scores = [dot(g, v[:, cols(h)], 1, 1) for g, h in zip(gs, hs)]
+        across = [dot(g, used[h].astype(BF16), 1, 1) for g, h in zip(gs, hs)]
+        values = [dot(mix[h], g, 0, 0) for g, h in zip(gs, hs)]
+        gms = [(a * wts[h]).astype(BF16) for a, h in zip(scores, hs)]
+        queries = [dot(m, k[:, cols(h)], 1, 0) for m, h in zip(gms, hs)]
+        keys = [dot(m, q[:, cols(h)], 0, 0) for m, h in zip(gms, hs)]
+        queries = [
+            (a + jnp.exp(run_col[h]) * b).astype(BF16) for a, b, h in zip(queries, across, hs)
+        ]
+        outs = []
+        for h in hs:
+            normed = ctx[h] * sq_acc[...]
+            opened = jax.nn.sigmoid(gate[:, cols(h)].astype(F32))
+            outs.append(
+                (
+                    (normed * gain_ref[:, cols(h)] * opened).astype(BF16),
+                    (gnorm[h] * normed * (1.0 - opened)).astype(BF16),
+                )
+            )
+        for h, a, b, c, (d, e) in zip(hs, queries, keys, values, outs):
+            gq[:, cols(h)] = a
+            gk_acc[h] = b
+            gv_acc[h] = c
+            att[:, cols(h)] = d
+            gg[:, cols(h)] = e
+
+    def finish_back(hs, states):
+        states = [state.astype(BF16) for state in states]
+        keys = [dot(v[:, cols(h)], a, 1, 1) for h, a in zip(hs, states)]
+        values = [dot(k[:, cols(h)], a, 1, 0) for h, a in zip(hs, states)]
+        done = []
+        for h, a, b in zip(hs, keys, values):
+            remain = remain_of(h)
+            done.append(((gk_acc[h] + remain * a).astype(BF16), (gv_acc[h] + remain * b).astype(BF16)))
+        for h, (a, b) in zip(hs, done):
+            gk[:, cols(h)] = a
+            gv[:, cols(h)] = b
 
     def chain_back(i):
         h = mine + i
@@ -311,44 +358,31 @@
             bx_copy(i, j).start()
             used_b[i, rows] = jnp.where(first, mid, came)
 
-    @pl.loop(0, half + last + LAG)
+    @pl.loop(0, groups + last + LAG)
     def _(t):
         step = t - (last - pair)
-        active = jnp.logical_and(step >= 0, step < half)
-
-        @pl.when(t < half)
-        def _():
-            gradient(mine + t)
+        active = jnp.logical_and(step >= 0, step < groups)
+        late = step - LAG
 
         @pl.when(active)
         def _():
-            chain_back(step)
-
-        @pl.when(t < half)
-        def _():
-            local_back(mine + t)
-            local_back(theirs + t)
+            for i in spread_of(0, step):
+                chain_back(i)
+
+        @pl.when(t < groups)
+        def _():
+            local_back(spread_of(mine, t) + spread_of(theirs, t))
 
         @pl.when(active)
         def _():
-            finish_back(mine + step, used_b[step])
-
-        late = step - LAG
-
-        @pl.when(jnp.logical_and(late >= 0, late < half))
-        def _():
-            for j in range(PARTS):
-                bx_copy(late, j).wait_recv()
-            finish_back(theirs + late, part_b[late])
-
-    stores = [
-        pltpu.make_async_copy(src, dst, out_sem.at[j])
-        for j, (src, dst) in enumerate(
-            [(att, att_hbm), (gq, gq_hbm), (gg, gg_hbm), (gk, gk_hbm), (gv, gv_hbm)]
-        )
-    ]
-    for store in stores:
-        store.start()
+            finish_back(spread_of(mine, step), [used_b[i] for i in spread_of(0, step)])
+
+        @pl.when(jnp.logical_and(late >= 0, late < groups))
+        def _():
+            for i in spread_of(0, late):
+                for j in range(PARTS):
+                    bx_copy(i, j).wait_recv()
+            finish_back(spread_of(theirs, late), [part_b[i] for i in spread_of(0, late)])
 
     dec_copy.wait_send()
     for copy in sum_copies:
@@ -370,25 +404,16 @@
             def _():
                 bz_copy(i, j).wait_send()
 
-    for store in stores:
-        store.wait()
-
-
-def deliver(rows, *refs):
-    sources, targets, staged, (in_sem, out_sem) = refs[:5], refs[5:10], refs[10:15], refs[15:]
-    loads, stores = [], []
-    for j in range(10):
-        part = pl.ds(j // 5 * rows, rows)
-        a, b, c = sources[j % 5].at[part], staged[j % 5].at[part], targets[j % 5].at[part]
-        loads.append(pltpu.make_async_copy(a, b, in_sem.at[j]))
-        stores.append(pltpu.make_async_copy(b, c, out_sem.at[j]))
-    for load in loads:
-        load.start()
-    for load, store in zip(loads, stores):
-        load.wait()
-        store.start()
-    for store in stores:
-        store.wait()
+
+def deliver(*refs):
+    sources, targets, sems = refs[:5], refs[5:10], refs[10]
+    copies = [
+        pltpu.make_async_copy(src, dst, sems.at[j]) for j, (src, dst) in enumerate(zip(sources, targets))
+    ]
+    for copy in copies:
+        copy.start()
+    for copy in copies:
+        copy.wait()
 
 
 def solution(mesh):
@@ -408,12 +433,11 @@
         dma = pltpu.SemaphoreType.DMA
         results = pl.pallas_call(
             functools.partial(kernel, n_seq, n_head, heads),
-            out_shape=[jax.ShapeDtypeStruct(wide, BF16)] * 5,
+            out_shape=[pltpu.VMEM(wide, BF16)] * 5,
             in_specs=[anywhere, anywhere, anywhere, vmem, anywhere, vmem, anywhere, anywhere],
-            out_specs=[anywhere] * 5,
+            out_specs=[vmem] * 5,
             scratch_shapes=[pltpu.VMEM(wide, BF16)] * 5
             + [states(heads)]
-            + [pltpu.VMEM(wide, BF16)] * 5
             + [
                 pltpu.VMEM((heads, BLK, HD), F32),
                 pltpu.VMEM((heads, BLK), F32),
@@ -435,7 +459,6 @@
                 pltpu.VMEM((8, BLK), F32),
                 pltpu.VMEM((n_head - 1, 8, BLK), F32),
                 dma((6,)),
-                dma((5,)),
                 dma,
                 dma,
                 dma((n_head - 1,)),
@@ -443,7 +466,7 @@
             ]
             + [dma((half * PARTS,))] * 12,
             compiler_params=pltpu.CompilerParams(
-                collective_id=0, has_side_effects=True, vmem_limit_bytes=56 * 1024 * 1024
+                collective_id=0, has_side_effects=True, vmem_limit_bytes=44 * 1024 * 1024
             ),
             cost_estimate=pl.CostEstimate(
                 flops=4_000_000_000, bytes_accessed=12_000_000, transcendentals=2_000_000
@@ -453,12 +476,11 @@
             out_gain.reshape(1, features), prior_state, out_grad,
         )
         return pl.pallas_call(
-            functools.partial(deliver, length // 2),
+            deliver,
             out_shape=[jax.ShapeDtypeStruct(wide, BF16)] * 5,
-            in_specs=[anywhere] * 5,
+            in_specs=[vmem] * 5,
             out_specs=[anywhere] * 5,
-            scratch_shapes=[pltpu.VMEM(wide, BF16)] * 5 + [dma((10,)), dma((10,))],
-            compiler_params=pltpu.CompilerParams(vmem_limit_bytes=60 * 1024 * 1024),
+            scratch_shapes=[dma((5,))],
             cost_estimate=pl.CostEstimate(flops=0, bytes_accessed=10_000_000, transcendentals=0),
         )(*results)
 

time: 86.7 us -> 93.1 us (1.074)
  local copies, waits for them, and re-layouts: 0 us -> 11.2 us
  Pallas kernels: 85.7 us -> 80.9 us
    unnamed x0 -> x22, local copies, waits for them, and re-layouts: none -> 11.2 us
    pallas_call x1, Pallas kernels: 81 us -> 76 us  [shards(): pl.pallas_call(functools.partial(kernel, n_seq, n_head, heads), out_shape...]
where the time goes in v3:
time: 93.1 us; the launch traced here: 92.8 us
  Pallas kernels  80.9 us (87%)
  local copies, waits for them, and re-layouts  11.2 us (12%)
    pallas_call x1, Pallas kernels, shards(): pl.pallas_call(functools.partial(kernel, n_seq, n_head, heads), out_shape...  76 us
    unnamed x22, local copies, waits for them, and re-layouts  11.2 us
    pallas_call x1, Pallas kernels, shards(): pl.pallas_call(deliver, out_shape=[jax.ShapeDtypeStruct(wide, BF16)] * 5,...  4.88 us

profile of v3, /device:TPU:0, one launch (start us, length us, event | category | flops | bytes accessed | tf_op | source)
XLA Modules:
  0.0 92.8 jit_solution(17062323298569495383)
XLA Ops:
  0.6 0.0 copy-start.5
  0.6 1.2 %copy-done.5 = bf16[256,2048]{1,0:T(8,128)(2,1)S(1)} copy-done((bf16[256,2048]{1,0:T(8,128)(2,1)S(1)}, bf16[256,2048]{1,0:T(8,128)(2,1)}, u32[]{:S(2)}) %copy-start.5) | copy-done | bytes 1048600
  1.9 0.0 copy-start.6
  1.9 1.2 %copy-done.6 = bf16[256,2048]{1,0:T(8,128)(2,1)S(1)} copy-done((bf16[256,2048]{1,0:T(8,128)(2,1)S(1)}, bf16[256,2048]{1,0:T(8,128)(2,1)}, u32[]{:S(2)}) %copy-start.6) | copy-done | bytes 1048600
  3.1 0.0 copy-start.7
  3.1 1.2 %copy-done.7 = bf16[256,2048]{1,0:T(8,128)(2,1)S(1)} copy-done((bf16[256,2048]{1,0:T(8,128)(2,1)S(1)}, bf16[256,2048]{1,0:T(8,128)(2,1)}, u32[]{:S(2)}) %copy-start.7) | copy-done | bytes 1048600
  4.3 0.0 copy-start.8
  4.3 1.2 %copy-done.8 = bf16[256,2048]{1,0:T(8,128)(2,1)S(1)} copy-done((bf16[256,2048]{1,0:T(8,128)(2,1)S(1)}, bf16[256,2048]{1,0:T(8,128)(2,1)}, u32[]{:S(2)}) %copy-start.8) | copy-done | bytes 1048600
  5.5 0.0 copy-start.9
  5.5 0.7 copy-done.9
  6.3 0.0 copy-start.10
  6.3 0.7 copy-done.10
  7.0 76.0 %shard_map.119 = (bf16[256,2048]{1,0:T(8,128)(2,1)S(1)}, bf16[256,2048]{1,0:T(8,128)(2,1)S(1)}, bf16[256,2048]{1,0:T(8,128)(2,1)S(1)}, bf16[256,2048]{1,0:T(8,128)(2,1)S(1)}, bf16[256,2048]{1,0:T(8,128)(2,1)S(1)}) custom-call(bf16[256,2048]{1,0:T(8,128)(2,1)S(1)} %copy-done.5, bf16[256,2048]{1,0:T(8,128)(2,1)S(1)} %copy-done.6, ...), custom_call_target="tpu_custom_call" | custom-call | flops 4000000000 | bytes 12000000 | tf_op jit(solution)/shard_map/pallas_call | solution.py:434
  82.9 0.0 copy-start
  83.0 1.0 %copy-done = bf16[256,2048]{1,0:T(8,128)(2,1)} copy-done((bf16[256,2048]{1,0:T(8,128)(2,1)}, bf16[256,2048]{1,0:T(8,128)(2,1)S(1)}, u32[]{:S(2)}) %copy-start) | copy-done | bytes 1048600
  83.9 0.0 copy-start.1
  83.9 1.0 %copy-done.1 = bf16[256,2048]{1,0:T(8,128)(2,1)} copy-done((bf16[256,2048]{1,0:T(8,128)(2,1)}, bf16[256,2048]{1,0:T(8,128)(2,1)S(1)}, u32[]{:S(2)}) %copy-start.1) | copy-done | bytes 1048600
  84.9 0.0 copy-start.2
  84.9 1.0 %copy-done.2 = bf16[256,2048]{1,0:T(8,128)(2,1)} copy-done((bf16[256,2048]{1,0:T(8,128)(2,1)}, bf16[256,2048]{1,0:T(8,128)(2,1)S(1)}, u32[]{:S(2)}) %copy-start.2) | copy-done | bytes 1048600
  85.9 0.0 copy-start.3
  85.9 1.0 %copy-done.3 = bf16[256,2048]{1,0:T(8,128)(2,1)} copy-done((bf16[256,2048]{1,0:T(8,128)(2,1)}, bf16[256,2048]{1,0:T(8,128)(2,1)S(1)}, u32[]{:S(2)}) %copy-start.3) | copy-done | bytes 1048600
  86.9 0.0 copy-start.4
  86.9 1.0 %copy-done.4 = bf16[256,2048]{1,0:T(8,128)(2,1)} copy-done((bf16[256,2048]{1,0:T(8,128)(2,1)}, bf16[256,2048]{1,0:T(8,128)(2,1)S(1)}, u32[]{:S(2)}) %copy-start.4) | copy-done | bytes 1048600
  87.9 4.9 %shard_map.120 = (bf16[256,2048]{1,0:T(8,128)(2,1)}, bf16[256,2048]{1,0:T(8,128)(2,1)}, bf16[256,2048]{1,0:T(8,128)(2,1)}, bf16[256,2048]{1,0:T(8,128)(2,1)}, bf16[256,2048]{1,0:T(8,128)(2,1)}) custom-call(bf16[256,2048]{1,0:T(8,128)(2,1)} %copy-done, bf16[256,2048]{1,0:T(8,128)(2,1)} %copy-done.1, bf16[256,2048]{1,0:T(8,128)(2,1)} %copy-done.2, ...), custom_call_target="tpu_custom_call" | custom-call | bytes 10000000 | tf_op jit(solution)/shard_map/pallas_call | solution.py:478
Async XLA Ops:
  0.6 1.2 %copy-start.5 = (bf16[256,2048]{1,0:T(8,128)(2,1)S(1)}, bf16[256,2048]{1,0:T(8,128)(2,1)}, u32[]{:S(2)}) copy-start(bf16[256,2048]{1,0:T(8,128)(2,1)} %q_hbm.1) | copy-start | bytes 3145732
  1.9 1.2 %copy-start.6 = (bf16[256,2048]{1,0:T(8,128)(2,1)S(1)}, bf16[256,2048]{1,0:T(8,128)(2,1)}, u32[]{:S(2)}) copy-start(bf16[256,2048]{1,0:T(8,128)(2,1)} %k_hbm.1) | copy-start | bytes 3145732
  3.1 1.2 %copy-start.7 = (bf16[256,2048]{1,0:T(8,128)(2,1)S(1)}, bf16[256,2048]{1,0:T(8,128)(2,1)}, u32[]{:S(2)}) copy-start(bf16[256,2048]{1,0:T(8,128)(2,1)} %v_hbm.1) | copy-start | bytes 3145732
  4.3 1.2 %copy-start.8 = (bf16[256,2048]{1,0:T(8,128)(2,1)S(1)}, bf16[256,2048]{1,0:T(8,128)(2,1)}, u32[]{:S(2)}) copy-start(bf16[256,2048]{1,0:T(8,128)(2,1)} %gate_hbm.1) | copy-start | bytes 3145732
  5.5 0.7 copy-start.9
  6.3 0.7 copy-start.10
  82.9 1.0 %copy-start = (bf16[256,2048]{1,0:T(8,128)(2,1)}, bf16[256,2048]{1,0:T(8,128)(2,1)S(1)}, u32[]{:S(2)}) copy-start(bf16[256,2048]{1,0:T(8,128)(2,1)S(1)} %get-tuple-element.10.refs_0_) | copy-start | bytes 3145732
  83.9 1.0 %copy-start.1 = (bf16[256,2048]{1,0:T(8,128)(2,1)}, bf16[256,2048]{1,0:T(8,128)(2,1)S(1)}, u32[]{:S(2)}) copy-start(bf16[256,2048]{1,0:T(8,128)(2,1)S(1)} %get-tuple-element.11.refs_1_) | copy-start | bytes 3145732
  84.9 1.0 %copy-start.2 = (bf16[256,2048]{1,0:T(8,128)(2,1)}, bf16[256,2048]{1,0:T(8,128)(2,1)S(1)}, u32[]{:S(2)}) copy-start(bf16[256,2048]{1,0:T(8,128)(2,1)S(1)} %get-tuple-element.12.refs_2_) | copy-start | bytes 3145732
  85.9 1.0 %copy-start.3 = (bf16[256,2048]{1,0:T(8,128)(2,1)}, bf16[256,2048]{1,0:T(8,128)(2,1)S(1)}, u32[]{:S(2)}) copy-start(bf16[256,2048]{1,0:T(8,128)(2,1)S(1)} %get-tuple-element.13.refs_3_) | copy-start | bytes 3145732
  86.9 1.0 %copy-start.4 = (bf16[256,2048]{1,0:T(8,128)(2,1)}, bf16[256,2048]{1,0:T(8,128)(2,1)S(1)}, u32[]{:S(2)}) copy-start(bf16[256,2048]{1,0:T(8,128)(2,1)S(1)} %get-tuple-element.14.refs_4_) | copy-start | bytes 3145732

commit v4 on v3

--- a/solution.py
+++ b/solution.py
@@ -11,7 +11,8 @@
 D = 8192
 HD = 128
 PARTS = 1
-LAG = 1
+LAG = 2
+HOP = 2
 GROUP = 2
 ROWS = HD // PARTS
 epsilon = 1e-06
@@ -27,14 +28,15 @@
 def kernel(
     n_seq, n_head, heads,
     q_hbm, k_hbm, v_hbm, ld_ref, gate_hbm, gain_ref, prior_hbm, og_hbm,
+    att_hbm, gq_hbm, gk_hbm, gv_hbm, gg_hbm,
+    q, k, v, gate, og, prior,
     att, gq, gk, gv, gg,
-    q, k, v, gate, og, prior,
     run_col, run_row, dec, dec_x,
     own, cross, enter, part, pass_z, pass_x, used,
     own_b, cross_b, enter_b, part_b, pass_z_b, pass_x_b, used_b,
     wts, mix, ctx, gnorm, grad, gk_acc, gv_acc,
     sq_acc, rd_acc, sums, sums_in,
-    in_sem, dec_send, dec_recv, sum_send, sum_recv,
+    in_sem, out_sem, dec_send, dec_recv, sum_send, sum_recv,
     s_send, s_recv, z_send, z_recv, x_send, x_recv,
     bs_send, bs_recv, bz_send, bz_recv, bx_send, bx_recv,
 ):
@@ -228,32 +230,29 @@
             x_copy(i, j).start()
             used[h, rows] = jnp.where(first, came, mid)
 
-    @pl.loop(0, groups + last + LAG)
+    @pl.loop(0, half + max(half, HOP * last + LAG))
     def _(t):
-        step = t - pair
-        active = jnp.logical_and(step >= 0, step < groups)
-        late = step - LAG
-
-        @pl.when(active)
-        def _():
-            for i in spread_of(0, step):
-                chain(i)
-
-        @pl.when(t < groups)
-        def _():
-            within(spread_of(mine, t) + spread_of(theirs, t))
-
-        @pl.when(active)
-        def _():
-            finish(spread_of(mine, step))
-
-        @pl.when(jnp.logical_and(late >= 0, late < groups))
-        def _():
-            for i in spread_of(0, late):
-                for j in range(PARTS):
-                    x_copy(i, j).wait_recv()
-                used[theirs + i] = part[i]
-            finish(spread_of(theirs, late))
+        step = t - HOP * pair
+        late = t - jnp.maximum(half, HOP * pair + LAG)
+
+        @pl.when(jnp.logical_and(step >= 0, step < half))
+        def _():
+            chain(step)
+
+        @pl.when(t < heads)
+        def _():
+            within([lax.rem(mine + t, heads)])
+
+        @pl.when(jnp.logical_and(step >= 0, step < half))
+        def _():
+            finish([mine + step])
+
+        @pl.when(jnp.logical_and(late >= 0, late < half))
+        def _():
+            for j in range(PARTS):
+                x_copy(late, j).wait_recv()
+            used[theirs + late] = part[late]
+            finish([theirs + late])
 
     sums[...] = jnp.zeros_like(sums)
     sums[0:1, :] = jnp.sum(sq_acc[...].T, axis=0, keepdims=True)
@@ -358,35 +357,51 @@
             bx_copy(i, j).start()
             used_b[i, rows] = jnp.where(first, mid, came)
 
-    @pl.loop(0, groups + last + LAG)
+    def stores(kind, h):
+        pairs = [(att, att_hbm), (gq, gq_hbm), (gg, gg_hbm), (gk, gk_hbm), (gv, gv_hbm)]
+        return [
+            pltpu.make_async_copy(pairs[j][0].at[:, cols(h)], pairs[j][1].at[:, cols(h)], out_sem.at[j, h])
+            for j in ((0, 1, 2), (3, 4), (0, 1, 2, 3, 4))[kind]
+        ]
+
+    @pl.loop(0, half + max(half, HOP * last + LAG))
     def _(t):
-        step = t - (last - pair)
-        active = jnp.logical_and(step >= 0, step < groups)
-        late = step - LAG
-
-        @pl.when(active)
-        def _():
-            for i in spread_of(0, step):
-                chain_back(i)
-
-        @pl.when(t < groups)
-        def _():
-            local_back(spread_of(mine, t) + spread_of(theirs, t))
-
-        @pl.when(active)
-        def _():
-            finish_back(spread_of(mine, step), [used_b[i] for i in spread_of(0, step)])
-
-        @pl.when(jnp.logical_and(late >= 0, late < groups))
-        def _():
-            for i in spread_of(0, late):
-                for j in range(PARTS):
-                    bx_copy(i, j).wait_recv()
-            finish_back(spread_of(theirs, late), [part_b[i] for i in spread_of(0, late)])
+        step = t - HOP * (last - pair)
+        late = t - jnp.maximum(half, HOP * (last - pair) + LAG)
+
+        @pl.when(jnp.logical_and(step >= 0, step < half))
+        def _():
+            chain_back(step)
+
+        @pl.when(t < heads)
+        def _():
+            h = lax.rem(mine + t, heads)
+            local_back([h])
+            for store in stores(0, h):
+                store.start()
+
+        @pl.when(jnp.logical_and(step >= 0, step < half))
+        def _():
+            finish_back([mine + step], [used_b[step]])
+            for store in stores(1, mine + step):
+                store.start()
+
+        @pl.when(jnp.logical_and(late >= 0, late < half))
+        def _():
+            for j in range(PARTS):
+                bx_copy(late, j).wait_recv()
+            finish_back([theirs + late], [part_b[late]])
+            for store in stores(1, theirs + late):
+                store.start()
 
     dec_copy.wait_send()
     for copy in sum_copies:
         copy.wait_send()
+
+    @pl.loop(0, heads)
+    def _(h):
+        for store in stores(2, h):
+            store.wait()
 
     @pl.loop(0, half)
     def _(i):
@@ -405,15 +420,21 @@
                 bz_copy(i, j).wait_send()
 
 
-def deliver(*refs):
-    sources, targets, sems = refs[:5], refs[5:10], refs[10]
-    copies = [
-        pltpu.make_async_copy(src, dst, sems.at[j]) for j, (src, dst) in enumerate(zip(sources, targets))
-    ]
-    for copy in copies:
-        copy.start()
-    for copy in copies:
-        copy.wait()
+def deliver(rows, *refs):
+    sources, targets, staged, (in_sem, out_sem) = refs[:5], refs[5:10], refs[10:15], refs[15:]
+    loads, stores = [], []
+    for j in range(10):
+        part = pl.ds(j // 5 * rows, rows)
+        a, b, c = sources[j % 5].at[part], staged[j % 5].at[part], targets[j % 5].at[part]
+        loads.append(pltpu.make_async_copy(a, b, in_sem.at[j]))
+        stores.append(pltpu.make_async_copy(b, c, out_sem.at[j]))
+    for load in loads:
+        load.start()
+    for load, store in zip(loads, stores):
+        load.wait()
+        store.start()
+    for store in stores:
+        store.wait()
 
 
 def solution(mesh):
@@ -433,11 +454,12 @@
         dma = pltpu.SemaphoreType.DMA
         results = pl.pallas_call(
             functools.partial(kernel, n_seq, n_head, heads),
-            out_shape=[pltpu.VMEM(wide, BF16)] * 5,
+            out_shape=[jax.ShapeDtypeStruct(wide, BF16)] * 5,
             in_specs=[anywhere, anywhere, anywhere, vmem, anywhere, vmem, anywhere, anywhere],
-            out_specs=[vmem] * 5,
+            out_specs=[anywhere] * 5,
             scratch_shapes=[pltpu.VMEM(wide, BF16)] * 5
             + [states(heads)]
+            + [pltpu.VMEM(wide, BF16)] * 5
             + [
                 pltpu.VMEM((heads, BLK, HD), F32),
                 pltpu.VMEM((heads, BLK), F32),
@@ -459,6 +481,7 @@
                 pltpu.VMEM((8, BLK), F32),
                 pltpu.VMEM((n_head - 1, 8, BLK), F32),
                 dma((6,)),
+                dma((5, heads)),
                 dma,
                 dma,
                 dma((n_head - 1,)),
@@ -466,7 +489,7 @@
             ]
             + [dma((half * PARTS,))] * 12,
             compiler_params=pltpu.CompilerParams(
-                collective_id=0, has_side_effects=True, vmem_limit_bytes=44 * 1024 * 1024
+                collective_id=0, has_side_effects=True, vmem_limit_bytes=60 * 1024 * 1024
             ),
             cost_estimate=pl.CostEstimate(
                 flops=4_000_000_000, bytes_accessed=12_000_000, transcendentals=2_000_000
@@ -476,11 +499,12 @@
             out_gain.reshape(1, features), prior_state, out_grad,
         )
         return pl.pallas_call(
-            deliver,
+            functools.partial(deliver, length // 2),
             out_shape=[jax.ShapeDtypeStruct(wide, BF16)] * 5,
-            in_specs=[vmem] * 5,
+            in_specs=[anywhere] * 5,
             out_specs=[anywhere] * 5,
-            scratch_shapes=[dma((5,))],
+            scratch_shapes=[pltpu.VMEM(wide, BF16)] * 5 + [dma((10,)), dma((10,))],
+            compiler_params=pltpu.CompilerParams(vmem_limit_bytes=60 * 1024 * 1024),
             cost_estimate=pl.CostEstimate(flops=0, bytes_accessed=10_000_000, transcendentals=0),
         )(*results)
 

time: 93.1 us -> 71.3 us (0.77)
  local copies, waits for them, and re-layouts: 11.2 us -> 0 us
  Pallas kernels: 80.9 us -> 70.3 us
    unnamed x22 -> x0, local copies, waits for them, and re-layouts: 11.2 us -> none
    pallas_call x1, Pallas kernels: 76 us -> 65.6 us  [shards(): pl.pallas_call(functools.partial(kernel, n_seq, n_head, heads), out_shape...]
where the time goes in v4:
time: 71.3 us; the launch traced here: 70.9 us
  Pallas kernels  70.3 us (99%)
    pallas_call x1, Pallas kernels, shards(): pl.pallas_call(functools.partial(kernel, n_seq, n_head, heads), out_shape...  65.6 us
    pallas_call x1, Pallas kernels, shards(): pl.pallas_call(functools.partial(deliver, length // 2), out_shape=[jax.Sh...  4.71 us

profile of v4, /device:TPU:0, one launch (start us, length us, event | category | flops | bytes accessed | tf_op | source)
XLA Modules:
  0.0 70.9 jit_solution(8263621587492337888)
XLA Ops:
  0.6 65.6 %shard_map.119 = (bf16[256,2048]{1,0:T(8,128)(2,1)}, bf16[256,2048]{1,0:T(8,128)(2,1)}, bf16[256,2048]{1,0:T(8,128)(2,1)}, bf16[256,2048]{1,0:T(8,128)(2,1)}, bf16[256,2048]{1,0:T(8,128)(2,1)}) custom-call(bf16[256,2048]{1,0:T(8,128)(2,1)} %q_hbm.1, bf16[256,2048]{1,0:T(8,128)(2,1)} %k_hbm.1, bf16[256,2048]{1,0:T(8,128)(2,1)} %v_hbm.1, f32[16,256]{1,0:T(8,128)} %bitcast.2, ...), custom_call_target="tpu_custom_call" | custom-call | flops 4000000000 | bytes 12000000 | tf_op jit(solution)/shard_map/pallas_call | solution.py:455
  66.2 4.7 %shard_map.120 = (bf16[256,2048]{1,0:T(8,128)(2,1)}, bf16[256,2048]{1,0:T(8,128)(2,1)}, bf16[256,2048]{1,0:T(8,128)(2,1)}, bf16[256,2048]{1,0:T(8,128)(2,1)}, bf16[256,2048]{1,0:T(8,128)(2,1)}) custom-call(bf16[256,2048]{1,0:T(8,128)(2,1)} %get-tuple-element.10.refs_0_, bf16[256,2048]{1,0:T(8,128)(2,1)} %get-tuple-element.11.refs_1_, ...), custom_call_target="tpu_custom_call" | custom-call | bytes 10000000 | tf_op jit(solution)/shard_map/pallas_call | solution.py:501

commit v5 on v4

--- a/solution.py
+++ b/solution.py
@@ -239,20 +239,25 @@
         def _():
             chain(step)
 
-        @pl.when(t < heads)
-        def _():
-            within([lax.rem(mine + t, heads)])
-
-        @pl.when(jnp.logical_and(step >= 0, step < half))
-        def _():
-            finish([mine + step])
-
-        @pl.when(jnp.logical_and(late >= 0, late < half))
-        def _():
-            for j in range(PARTS):
-                x_copy(late, j).wait_recv()
-            used[theirs + late] = part[late]
-            finish([theirs + late])
+        def closes(n):
+            return (n >= 0) & (n < half) & (lax.rem(n + GROUP, GROUP) == GROUP - 1)
+
+        @pl.when((t < heads) & (lax.rem(t, GROUP) == 0))
+        def _():
+            h = lax.rem(mine + t, heads)
+            within([h + i for i in range(GROUP)])
+
+        @pl.when(closes(step))
+        def _():
+            finish([mine + step - i for i in range(GROUP)])
+
+        @pl.when(closes(late))
+        def _():
+            for i in range(GROUP):
+                for j in range(PARTS):
+                    x_copy(late - i, j).wait_recv()
+                used[theirs + late - i] = part[late - i]
+            finish([theirs + late - i for i in range(GROUP)])
 
     sums[...] = jnp.zeros_like(sums)
     sums[0:1, :] = jnp.sum(sq_acc[...].T, axis=0, keepdims=True)
@@ -373,26 +378,35 @@
         def _():
             chain_back(step)
 
-        @pl.when(t < heads)
-        def _():
-            h = lax.rem(mine + t, heads)
-            local_back([h])
-            for store in stores(0, h):
-                store.start()
-
-        @pl.when(jnp.logical_and(step >= 0, step < half))
-        def _():
-            finish_back([mine + step], [used_b[step]])
-            for store in stores(1, mine + step):
-                store.start()
-
-        @pl.when(jnp.logical_and(late >= 0, late < half))
-        def _():
-            for j in range(PARTS):
-                bx_copy(late, j).wait_recv()
-            finish_back([theirs + late], [part_b[late]])
-            for store in stores(1, theirs + late):
-                store.start()
+        def closes(n):
+            return (n >= 0) & (n < half) & (lax.rem(n + GROUP, GROUP) == GROUP - 1)
+
+        @pl.when((t < heads) & (lax.rem(t, GROUP) == 0))
+        def _():
+            hs = [lax.rem(mine + t, heads) + i for i in range(GROUP)]
+            local_back(hs)
+            for h in hs:
+                for store in stores(0, h):
+                    store.start()
+
+        @pl.when(closes(step))
+        def _():
+            hs = [step - i for i in range(GROUP)]
+            finish_back([mine + i for i in hs], [used_b[i] for i in hs])
+            for i in hs:
+                for store in stores(1, mine + i):
+                    store.start()
+
+        @pl.when(closes(late))
+        def _():
+            hs = [late - i for i in range(GROUP)]
+            for i in hs:
+                for j in range(PARTS):
+                    bx_copy(i, j).wait_recv()
+            finish_back([theirs + i for i in hs], [part_b[i] for i in hs])
+            for i in hs:
+                for store in stores(1, theirs + i):
+                    store.start()
 
     dec_copy.wait_send()
     for copy in sum_copies:

time: 71.3 us -> 70.7 us (level)
  no operation moved by 1% of the time
where the time goes in v5:
time: 70.7 us; the launch traced here: 70.4 us
  Pallas kernels  69.7 us (99%)
    pallas_call x1, Pallas kernels, shards(): pl.pallas_call(functools.partial(kernel, n_seq, n_head, heads), out_shape...  65 us
    pallas_call x1, Pallas kernels, shards(): pl.pallas_call(functools.partial(deliver, length // 2), out_shape=[jax.Sh...  4.71 us

profile of v5, /device:TPU:0, one launch (start us, length us, event | category | flops | bytes accessed | tf_op | source)
XLA Modules:
  0.0 70.4 jit_solution(12643700320989959734)
XLA Ops:
  0.6 65.0 %shard_map.119 = (bf16[256,2048]{1,0:T(8,128)(2,1)}, bf16[256,2048]{1,0:T(8,128)(2,1)}, bf16[256,2048]{1,0:T(8,128)(2,1)}, bf16[256,2048]{1,0:T(8,128)(2,1)}, bf16[256,2048]{1,0:T(8,128)(2,1)}) custom-call(bf16[256,2048]{1,0:T(8,128)(2,1)} %q_hbm.1, bf16[256,2048]{1,0:T(8,128)(2,1)} %k_hbm.1, bf16[256,2048]{1,0:T(8,128)(2,1)} %v_hbm.1, f32[16,256]{1,0:T(8,128)} %bitcast.2, ...), custom_call_target="tpu_custom_call" | custom-call | flops 4000000000 | bytes 12000000 | tf_op jit(solution)/shard_map/pallas_call | solution.py:469
  65.7 4.7 %shard_map.120 = (bf16[256,2048]{1,0:T(8,128)(2,1)}, bf16[256,2048]{1,0:T(8,128)(2,1)}, bf16[256,2048]{1,0:T(8,128)(2,1)}, bf16[256,2048]{1,0:T(8,128)(2,1)}, bf16[256,2048]{1,0:T(8,128)(2,1)}) custom-call(bf16[256,2048]{1,0:T(8,128)(2,1)} %get-tuple-element.10.refs_0_, bf16[256,2048]{1,0:T(8,128)(2,1)} %get-tuple-element.11.refs_1_, ...), custom_call_target="tpu_custom_call" | custom-call | bytes 10000000 | tf_op jit(solution)/shard_map/pallas_call | solution.py:515
